TPU v7x, 128 devices: a whole 4x4x4 slice. The times are simulated.
128 devices in a mesh: seq: 32 (over z, x, core), head: 4 (over y).
Axes of the slice: x: 4, y: 4, z: 4, core: 2. Of those that a mesh axis runs over, the one named last changes fastest.
Arguments:
- queries: bfloat16 [32768, 4096], P('seq', 'head'), may hold values from -6 to 6
- keys: bfloat16 [32768, 4096], P('seq', 'head'), may hold values from -6 to 6
- values: bfloat16 [32768, 4096], P('seq', 'head'), may hold values from -6 to 6
- out_weight: bfloat16 [4096, 4096], P('head', 'seq'), may hold values from -0.09375 to 0.09375
Outputs:
- mixed: bfloat16 [32768, 4096], P('seq', 'head')
All inputs are finite; a program needn't handle non-finite values.
Results may differ from a plain program's by a relative error of at most 0.015.
Values may be sent and summed in bfloat16 or wider, within the bound.
No kernel may reach another device: no remote copies, remote signals or barrier semaphores. Data moves between devices by JAX's collectives and lax.ppermute only.
A program may use at most 128 MiB of HBM per device.

v0:
```python
import functools

import jax
import jax.numpy as jnp
from jax import lax
from jax.experimental import pallas as pl
from jax.experimental.pallas import tpu as pltpu
from jax.sharding import PartitionSpec as P

HEAD_DIM = 128
BLOCK = 512
EPSILON = 1e-06
AXES = ("seq", "head")
NZ, NX, NC, NY = 4, 4, 2, 4
OFFSETS = (0, 1, -1, 2)
QROWS = 256
CHUNKS = ((0, 128), (128, 128), (256, 256), (512, 256), (768, 128), (896, 128))
VMEM_LIMIT = 10 * 1024 * 1024
COST = pl.CostEstimate(flops=1, bytes_accessed=1, transcendentals=0)


def route(target):
    pairs = []
    for z in range(NZ):
        for x in range(NX):
            for c in range(NC):
                for y in range(NY):
                    z2, x2, c2, y2 = target(z, x, c, y)
                    source = ((z * NX + x) * NC + c) * NY + y
                    to = (((z2 % NZ) * NX + x2 % NX) * NC + c2) * NY + y2
                    pairs.append((source, to))
    return pairs


def send(array, target):
    return lax.ppermute(array, AXES, route(target))


def params():
    return pltpu.CompilerParams(vmem_limit_bytes=VMEM_LIMIT)


def feature(source):
    wide = source.astype(jnp.float32)
    return jnp.where(wide > 0, wide + 1.0, jnp.exp(jnp.minimum(wide, 0.0))).astype(jnp.bfloat16)


def state_kernel(keys_hbm, values_hbm, feat_ref, total_ref, first_ref, keys, values, arrived):
    groups, _, width = keys.shape
    copies = []
    for group in range(groups):
        columns = slice(group * width, (group + 1) * width)
        for index, (source, target) in enumerate(((keys_hbm, keys), (values_hbm, values))):
            copies.append(
                pltpu.make_async_copy(
                    source.at[:, columns], target.at[group], arrived.at[group, index]
                )
            )
            copies[-1].start()
    for group in range(groups):
        copies[2 * group].wait()
        copies[2 * group + 1].wait()
        for inner in range(width // HEAD_DIM):
            head = group * (width // HEAD_DIM) + inner
            here = slice(inner * HEAD_DIM, (inner + 1) * HEAD_DIM)
            feat = feature(keys[group, :, here])
            feat_ref[:, head * HEAD_DIM : (head + 1) * HEAD_DIM] = feat
            sums = []
            for block in range(2):
                rows = slice(block * BLOCK, (block + 1) * BLOCK)
                sums.append(
                    lax.dot_general(
                        feat[rows],
                        values[group, rows, here],
                        (((0,), (0,)), ((), ())),
                        preferred_element_type=jnp.float32,
                    )
                )
            first_ref[head] = sums[0]
            total_ref[head] = (sums[0] + sums[1]).astype(jnp.bfloat16)


def states(keys, values):
    tokens, features = keys.shape
    heads = features // HEAD_DIM
    groups = 4
    buffer = pltpu.VMEM((groups, tokens, features // groups), jnp.bfloat16)
    return pl.pallas_call(
        state_kernel,
        in_specs=[pl.BlockSpec(memory_space=pltpu.HBM)] * 2,
        out_shape=[
            jax.ShapeDtypeStruct((tokens, features), jnp.bfloat16),
            jax.ShapeDtypeStruct((heads, HEAD_DIM, HEAD_DIM), jnp.bfloat16),
            jax.ShapeDtypeStruct((heads, HEAD_DIM, HEAD_DIM), jnp.float32),
        ],
        scratch_shapes=[buffer, buffer, pltpu.SemaphoreType.DMA((groups, 2))],
        compiler_params=params(),
        cost_estimate=COST,
        name="states",
    )(keys, values)


def local_kernel(queries_ref, feat_ref, values_ref, local_ref, query_feat_ref):
    rows = queries_ref.shape[0]
    span = feat_ref.shape[0]
    row = lax.broadcasted_iota(jnp.int32, (rows, rows), 0)
    column = lax.broadcasted_iota(jnp.int32, (rows, rows), 1)
    causal = column <= row
    for head in range(queries_ref.shape[1] // HEAD_DIM):
        columns = slice(head * HEAD_DIM, (head + 1) * HEAD_DIM)
        query_feat = feature(queries_ref[:, columns])
        query_feat_ref[:, columns] = query_feat
        scores = lax.dot_general(
            query_feat,
            feat_ref[:, columns],
            (((1,), (1,)), ((), ())),
            preferred_element_type=jnp.float32,
        )
        diagonal = jnp.where(causal, scores[:, span - rows :], 0.0).astype(jnp.bfloat16)
        out = jnp.dot(
            diagonal, values_ref[span - rows :, columns], preferred_element_type=jnp.float32
        )
        if span > rows:
            out += jnp.dot(
                scores[:, : span - rows].astype(jnp.bfloat16),
                values_ref[: span - rows, columns],
                preferred_element_type=jnp.float32,
            )
        local_ref[:, columns] = out


def local_part(queries, key_feat, values, index):
    features = queries.shape[1]
    width = features // 2
    span = QROWS * (index % 2 + 1)
    first = (index // 2) * (BLOCK // span)
    rows = pl.BlockSpec((QROWS, width), lambda i: (index, i))
    source = pl.BlockSpec((span, width), lambda i: (first, i))
    out = pl.BlockSpec((QROWS, width), lambda i: (0, i))
    return pl.pallas_call(
        local_kernel,
        grid=(features // width,),
        in_specs=[rows, source, source],
        out_specs=[out, out],
        out_shape=[
            jax.ShapeDtypeStruct((QROWS, features), jnp.float32),
            jax.ShapeDtypeStruct((QROWS, features), jnp.bfloat16),
        ],
        compiler_params=params(),
        cost_estimate=COST,
        name="local_part",
    )(queries, key_feat, values)


def norm_kernel(local_ref, query_feat_ref, start_ref, normed_ref):
    for head in range(local_ref.shape[1] // HEAD_DIM):
        columns = slice(head * HEAD_DIM, (head + 1) * HEAD_DIM)
        combined = local_ref[:, columns] + jnp.dot(
            query_feat_ref[:, columns], start_ref[0, head], preferred_element_type=jnp.float32
        )
        mean = jnp.mean(combined * combined, axis=-1, keepdims=True)
        normed_ref[:, columns] = (combined * lax.rsqrt(mean + EPSILON)).astype(jnp.bfloat16)


def norm_part(local, query_feat, start, row, rows):
    features = local.shape[1]
    heads = features // HEAD_DIM
    block = row // BLOCK
    place = (row % QROWS) // rows
    spec = pl.BlockSpec((rows, features), lambda i: (place, 0))
    return pl.pallas_call(
        norm_kernel,
        grid=(1,),
        in_specs=[
            spec,
            spec,
            pl.BlockSpec((1, heads, HEAD_DIM, HEAD_DIM), lambda i: (block, 0, 0, 0)),
        ],
        out_specs=pl.BlockSpec((rows, features), lambda i: (0, 0)),
        out_shape=jax.ShapeDtypeStruct((rows, features), jnp.bfloat16),
        compiler_params=params(),
        cost_estimate=COST,
        name="norm_part",
    )(local, query_feat, start)


def position():
    seq = lax.axis_index("seq")
    return seq // (NX * NC), (seq // NC) % NX, seq % NC, lax.axis_index("head")


def after(value, *done):
    return lax.optimization_barrier((value, *done))[0]


def small(body, shapes, *operands, name):
    return pl.pallas_call(
        body,
        out_shape=shapes,
        compiler_params=params(),
        cost_estimate=COST,
        name=name,
    )(*operands)


def assemble_kernel(home, blocks, *refs):
    out_ref, arrived = refs[-2:]
    z, x, c, y = position()
    piece_rows, piece_columns = refs[0].shape[-2:]
    copies = []
    for number, (index, inner, place) in enumerate(blocks):
        from_z, from_x, core = place(z, x, c)
        kind = jnp.bitwise_xor(from_z, y)
        slot = jnp.where((kind == 0) | (kind == 3), 0, 1)
        second = jnp.where((kind < 2) == (home == 0), 0, 1)
        column = (from_x * NC + core) * piece_columns
        copies.append(
            pltpu.make_async_copy(
                refs[index].at[inner],
                out_ref.at[
                    slot,
                    pl.ds(pl.multiple_of(second * piece_rows, piece_rows), piece_rows),
                    pl.ds(pl.multiple_of(column, piece_columns), piece_columns),
                ],
                arrived.at[number],
            )
        )
    for copy in copies:
        copy.start()
    for copy in copies:
        copy.wait()


def assemble(home, blocks, *pieces):
    side = 2 * pieces[0].shape[-2]
    return pl.pallas_call(
        functools.partial(assemble_kernel, home, blocks),
        in_specs=[pl.BlockSpec(memory_space=pl.ANY)] * len(pieces),
        out_specs=pl.BlockSpec(memory_space=pl.ANY),
        out_shape=jax.ShapeDtypeStruct((2, side, side), jnp.bfloat16),
        scratch_shapes=[pltpu.SemaphoreType.DMA((len(blocks),))],
        compiler_params=params(),
        cost_estimate=COST,
        name="assemble",
    )(*pieces)


def project_kernel(normed_ref, peer_ref, weight_ref, out_ref, *, received_ref=None):
    total = jnp.dot(normed_ref[...], weight_ref[0], preferred_element_type=jnp.float32)
    total += jnp.dot(peer_ref[...], weight_ref[1], preferred_element_type=jnp.float32)
    if received_ref is not None:
        total += received_ref[...].astype(jnp.float32)
    out_ref[...] = total.astype(jnp.bfloat16)


def project(normed, peer, weight, received=None, row=0, tokens=0, target=None):
    rows, features = normed.shape
    own = received is not None
    chunk = pl.BlockSpec((rows, features), lambda i: (0, 0))
    place = row // rows if own else 0
    operands = [normed, peer, weight]
    specs = [chunk, chunk, pl.BlockSpec(weight.shape, lambda i: (0, 0, 0))]
    aliases = {}
    if own:
        operands.append(received)
        specs.append(chunk)
    if target is not None:
        aliases = {len(operands): 0}
        operands.append(target)
        specs.append(pl.BlockSpec(memory_space=pl.ANY))

    def body(*refs):
        project_kernel(*refs[:3], refs[-1], received_ref=refs[3] if own else None)

    return pl.pallas_call(
        body,
        grid=(1,),
        in_specs=specs,
        out_specs=pl.BlockSpec((rows, features), lambda i: (place, 0)),
        out_shape=jax.ShapeDtypeStruct((tokens if own else rows, features), jnp.bfloat16),
        input_output_aliases=aliases,
        compiler_params=params(),
        cost_estimate=COST,
        name="project_own" if own else "project_other",
    )(*operands)


def other_core(z, x, c, y):
    return z, x, 1 - c, y


def along_x(away, z, x, c, y):
    return z, x - away, c, y


def along_z(away, z, x, c, y):
    return z - away, x, c, y


def chip_kernel(total_ref, peer_ref, wide_ref, chip_ref):
    half = chip_ref.shape[0]
    mine = pl.ds(position()[2] * half, half)
    wide = total_ref[mine].astype(jnp.float32) + peer_ref[mine].astype(jnp.float32)
    wide_ref[...] = wide
    chip_ref[...] = wide.astype(jnp.bfloat16)


def step_kernel(axis, bit, *refs):
    wide_ref, other_ref, next_wide_ref, next_ref, earlier_out_ref = refs[0], *refs[-4:]
    place = position()[axis]
    other = other_ref[...].astype(jnp.float32)
    wide = wide_ref[...] + other
    earlier = jnp.where(jnp.bitwise_and(place, bit) != 0, other, 0.0)
    if len(refs) == 6:
        earlier += refs[1][...]
    next_wide_ref[...] = wide
    next_ref[...] = wide.astype(jnp.bfloat16)
    earlier_out_ref[...] = earlier


def last_kernel(earlier_ref, other_ref, half_ref):
    place = position()[0]
    other = other_ref[...].astype(jnp.float32)
    half_ref[...] = (earlier_ref[...] + jnp.where(place >= 2, other, 0.0)).astype(jnp.bfloat16)


def start_kernel(mine_ref, other_ref, peer_ref, first_ref, start_ref):
    core = position()[2]
    half = mine_ref.shape[0]
    for place in range(2):
        heads = slice(place * half, (place + 1) * half)
        carried = jnp.where(
            core == place, mine_ref[...].astype(jnp.float32), other_ref[...].astype(jnp.float32)
        )
        carried += jnp.where(core == 1, peer_ref[heads].astype(jnp.float32), 0.0)
        start_ref[0, heads] = carried.astype(jnp.bfloat16)
        start_ref[1, heads] = (carried + first_ref[heads]).astype(jnp.bfloat16)


def home(z, y):
    return (z, y) if (z ^ y) in (0, 3) else (z ^ 1, y ^ 1)


def item_kernel(a_ref, b_ref, own_ref, other_ref):
    z, _, _, y = position()
    far = jnp.bitwise_xor(z, y) >= 2
    own_ref[...] = jnp.where(far, b_ref[...], a_ref[...])
    other_ref[...] = jnp.where(far, a_ref[...], b_ref[...])


def spread_weight(weight):
    rows = weight.shape[0] // 2

    def to(second, z, x, c, y):
        z, y = home(z, y)
        return (z ^ 3 if second else z), x, c, y

    parts = [weight[:rows], weight[rows:]]
    return parts[0], [send(part, functools.partial(to, i)) for i, part in enumerate(parts)]


def first_moves(item):
    return [item] + [send(item, functools.partial(line_move, True, away)) for away in OFFSETS[1:]]


def second_moves(line):
    return [line] + [send(line, functools.partial(line_move, False, away)) for away in OFFSETS[1:]]


def line_move(first, away, z, x, c, y):
    return along_x(away, z, x, c, y) if (c == 0) == first else along_z(away, z, x, c, y)


def line_place(mine, outer, inner, z, x, c):
    core = c if mine else 1 - c
    from_z = lax.rem(z + jnp.where(core == 0, outer, inner) + NZ, NZ)
    from_x = lax.rem(x + jnp.where(core == 0, inner, outer) + NX, NX)
    return from_z, from_x, core


def pair_place(mine, outer, inner, z, x, c):
    from_z, from_x, core = line_place(True, outer, inner, z, x, c)
    return from_z, from_x, core if mine else 1 - core


PAIR_BLOCKS = [
    (index, (inner, side), functools.partial(pair_place, side == 0, OFFSETS[index], OFFSETS[inner]))
    for index in range(4)
    for inner in range(4)
    for side in range(2)
]

LINE_BLOCKS = [
    (index, inner, functools.partial(line_place, index < 4, OFFSETS[index % 4], OFFSETS[inner]))
    for index in range(8)
    for inner in range(4)
]


def on_device(queries, keys, values, out_weight):
    tokens = queries.shape[0]

    ready, parts = spread_weight(out_weight)
    key_feat, total, first = states(after(keys, ready), values)
    heads = total.shape[0]
    half = jax.ShapeDtypeStruct((heads // 2, HEAD_DIM, HEAD_DIM), jnp.bfloat16)
    wide_half = jax.ShapeDtypeStruct(half.shape, jnp.float32)

    total = after(total, *parts)
    peer = send(total, other_core)
    item = jax.ShapeDtypeStruct(parts[0].shape, parts[0].dtype)
    own_item, other_item = small(
        item_kernel, [item, item], *after(tuple(parts), total), name="weight_items"
    )

    wide, chip = small(chip_kernel, [wide_half, half], total, peer, name="chip_sum")
    other_chip = send(chip, lambda z, x, c, y: (z, x ^ 1, c, y))
    line = first_moves(after(other_item, chip))
    local = [local_part(after(queries, chip), key_feat, values, 0)]
    wide, chip, earlier = small(
        functools.partial(step_kernel, 1, 1),
        [wide_half, half, wide_half],
        wide,
        after(other_chip, local[0][0]),
        name="step_x",
    )
    other_chip = send(chip, lambda z, x, c, y: (z, 3 - x, c, y))
    wide, chip, earlier = small(
        functools.partial(step_kernel, 1, 2),
        [wide_half, half, wide_half],
        wide,
        earlier,
        other_chip,
        name="step_x2",
    )
    own_pair = jnp.stack([own_item, send(after(own_item, chip), other_core)])
    other_chip = send(chip, lambda z, x, c, y: (z ^ 1, x, c, y))
    other_chip = after(other_chip, own_pair)
    wide, chip, earlier = small(
        functools.partial(step_kernel, 0, 1),
        [wide_half, half, wide_half],
        wide,
        earlier,
        other_chip,
        name="step_z",
    )
    other_chip = send(chip, lambda z, x, c, y: (3 - z, x, c, y))
    line = jnp.stack(after(tuple(line), chip))
    lines = second_moves(line)
    my_half = small(last_kernel, half, earlier, after(other_chip, line), name="step_z2")
    other_half = send(my_half, other_core)
    start = small(
        start_kernel,
        jax.ShapeDtypeStruct((2, heads, HEAD_DIM, HEAD_DIM), jnp.bfloat16),
        my_half,
        other_half,
        peer,
        first,
        name="start_states",
    )

    normed, peers, partial = [], [], []

    def norm(index, *done):
        place, rows = CHUNKS[index]
        number = place // QROWS
        if number == len(local):
            local.append(local_part(after(queries, *done), key_feat, values, number))
        query_feat = after(local[number][1], *done) if done else local[number][1]
        normed.append(norm_part(local[number][0], query_feat, start, place, rows))
        peers.append(send(normed[-1], lambda z, x, c, y: (z, x, c, y ^ 1)))

    def other(index):
        partial.append(project(normed[index], peers[index], weight))
        return partial[-1]

    received = []

    def reply(index):
        received.append(send(partial[index], lambda z, x, c, y: (z, x, c, 3 - y)))

    received = []

    def reply(index):
        received.append(send(partial[index], lambda z, x, c, y: (z, x, c, 3 - y)))

    norm(0)
    norm(1, normed[0])
    norm(2, normed[1])
    own_line = first_moves(after(own_pair, normed[0]))
    lines = list(after(tuple(lines), peers[0], normed[2]))
    lines += [send(piece, other_core) for piece in lines]
    weight = assemble(1, LINE_BLOCKS, *lines)
    other(0)
    reply(0)
    peers[1] = after(peers[1], partial[0])
    other(1)
    reply(1)
    own_lines = second_moves(jnp.stack(after(tuple(own_line), partial[1])))
    norm(3, partial[1])
    peers[2] = after(peers[2], received[0], received[1], normed[3])
    other(2)
    reply(2)
    norm(4, partial[2])
    norm(5, normed[4])
    peers[3] = after(peers[3], normed[5])
    other(3)
    reply(3)
    peers[4] = after(peers[4], received[2], partial[3])
    other(4)
    reply(4)
    own_weight = assemble(0, PAIR_BLOCKS, *after(tuple(own_lines), partial[4]))
    out = None

    def own(index, *done):
        row = CHUNKS[index][0]
        back = after(received[index], *done) if done else received[index]
        return project(normed[index], peers[index], own_weight, back, row, tokens, out)

    for index in range(3):
        out = own(index)
    peers[5] = after(peers[5], received[3], out)
    other(5)
    reply(5)
    out = own(3, partial[5])
    out = own(4)
    return own(5)


def solution(mesh):
    in_specs = (P("seq", "head"), P("seq", "head"), P("seq", "head"), P("head", "seq"))
    out_specs = P("seq", "head")
    return jax.shard_map(
        on_device, mesh=mesh, in_specs=in_specs, out_specs=out_specs, check_vma=False
    )
```

profile of v0, /device:TPU:0, one launch (start us, length us, event | category | flops | bytes accessed | tf_op | source)
XLA Modules:
  0.0 124.3 jit_solution(1042393104123431377)
XLA Ops:
  1.7 4.2 %collective-permute-start.1 = (bf16[512,128]{1,0:T(8,128)(2,1)S(1)}, bf16[512,128]{1,0:T(8,128)(2,1)S(1)}, u32[]{:S(2)}, u32[]{:S(2)}) collective-permute-start(bf16[512,128]{1,0:T(8,128)(2,1)S(1)} %get-tuple-element.133), channel_id=1, source_target_pairs={{0,96},{1,64},{2,67},{3,99},{4,100},{5,68},{6,71},{7,103},{8,104},... | collective-permute-start | bytes 393224 | tf_op jit(solution)/shard_map/ppermute | solution.py:36
  9.1 2.8 %states.1 = (bf16[1024,1024]{1,0:T(8,128)(2,1)S(1)}, bf16[8,128,128]{2,1,0:T(8,128)(2,1)S(1)}, f32[8,128,128]{2,1,0:T(8,128)S(1)}) custom-call(bf16[1024,1024]{1,0:T(8,128)(2,1)S(1)} %copy-done.3, bf16[1024,1024]{1,0:T(8,128)(2,1)S(1)} %copy-done), custom_call_target="tpu_custom_call" | custom-call | flops 1 | bytes 1 | tf_op jit(solution)/shard_map/states/pallas_call | solution.py:88
  16.7 2.5 %collective-permute-done.3.refs_1_ = bf16[4,128,128]{2,1,0:T(8,128)(2,1)S(1)} collective-permute-done((bf16[4,128,128]{2,1,0:T(8,128)(2,1)S(1)}, bf16[4,128,128]{2,1,0:T(8,128)(2,1)S(1)}, u32[]{:S(2)}, u32[]{:S(2)}) %collective-permute-start.3) | collective-permute-done | bytes 131104 | tf_op jit(solution)/shard_map/ppermute | solution.py:36
  19.2 2.8 %collective-permute-start.4 = (bf16[4,128,128]{2,1,0:T(8,128)(2,1)S(1)}, bf16[4,128,128]{2,1,0:T(8,128)(2,1)S(1)}, u32[]{:S(2)}, u32[]{:S(2)}) collective-permute-start(bf16[4,128,128]{2,1,0:T(8,128)(2,1)S(1)} %get-tuple-element.81), channel_id=1, source_target_pairs={{0,24},{1,25},{2,26},{3,27},{4,28},{5,29},{6,30},{7,31},{8,16},{9,... | collective-permute-start | bytes 393224 | tf_op jit(solution)/shard_map/ppermute | solution.py:36
  22.2 3.3 %collective-permute-done.4.refs_2_ = bf16[4,128,128]{2,1,0:T(8,128)(2,1)S(1)} collective-permute-done((bf16[4,128,128]{2,1,0:T(8,128)(2,1)S(1)}, bf16[4,128,128]{2,1,0:T(8,128)(2,1)S(1)}, u32[]{:S(2)}, u32[]{:S(2)}) %collective-permute-start.4) | collective-permute-done | bytes 131104 | tf_op jit(solution)/shard_map/ppermute | solution.py:36
  25.7 3.5 %collective-permute-start.5 = (bf16[4,128,128]{2,1,0:T(8,128)(2,1)S(1)}, bf16[4,128,128]{2,1,0:T(8,128)(2,1)S(1)}, u32[]{:S(2)}, u32[]{:S(2)}) collective-permute-start(bf16[4,128,128]{2,1,0:T(8,128)(2,1)S(1)} %get-tuple-element.84), channel_id=1, source_target_pairs={{0,32},{1,33},{2,34},{3,35},{4,36},{5,37},{6,38},{7,39},{8,40},{9,... | collective-permute-start | bytes 393224 | tf_op jit(solution)/shard_map/ppermute | solution.py:36
  34.2 2.1 %collective-permute-start.7 = (bf16[4,128,128]{2,1,0:T(8,128)(2,1)S(1)}, bf16[4,128,128]{2,1,0:T(8,128)(2,1)S(1)}, u32[]{:S(2)}, u32[]{:S(2)}) collective-permute-start(bf16[4,128,128]{2,1,0:T(8,128)(2,1)S(1)} %get-tuple-element.91), channel_id=1, source_target_pairs={{0,96},{1,97},{2,98},{3,99},{4,100},{5,101},{6,102},{7,103},{8,104... | collective-permute-start | bytes 393224 | tf_op jit(solution)/shard_map/ppermute | solution.py:36
  38.3 2.2 %collective-permute-start.14 = (bf16[4,512,128]{2,1,0:T(8,128)(2,1)S(1)}, bf16[4,512,128]{2,1,0:T(8,128)(2,1)S(1)}, u32[]{:S(2)}, u32[]{:S(2)}) collective-permute-start(bf16[4,512,128]{2,1,0:T(8,128)(2,1)S(1)} %pad_maximum_fusion.1.refs_0_), channel_id=1, source_target_pairs={{0,96},{1,97},{2,98},{3,99},{4,28},{5,29},{6,30},{7,31},{8,104},{9... | collective-permute-start | bytes 1572872 | tf_op jit(solution)/shard_map/ppermute | solution.py:36
  44.1 2.3 %collective-permute-start.13 = (bf16[128,1024]{1,0:T(8,128)(2,1)S(1)}, bf16[128,1024]{1,0:T(8,128)(2,1)S(1)}, u32[]{:S(2)}, u32[]{:S(2)}) collective-permute-start(bf16[128,1024]{1,0:T(8,128)(2,1)S(1)} %norm_part.6.refs_0_), channel_id=1, source_target_pairs={{0,1},{1,0},{2,3},{3,2},{4,5},{5,4},{6,7},{7,6},{8,9},{9,8},{10,11... | collective-permute-start | bytes 786440 | tf_op jit(solution)/shard_map/ppermute | solution.py:36
  46.8 2.3 %local_part.5 = (f32[256,1024]{1,0:T(8,128)S(1)}, bf16[256,1024]{1,0:T(8,128)(2,1)S(1)}) custom-call(bf16[1024,1024]{1,0:T(8,128)(2,1)S(1)} %copy-done.2, bf16[1024,1024]{1,0:T(8,128)(2,1)S(1)} %get-tuple-element.74.feat_ref, bf16[1024,1024]{1,0:T(8,128)(2,1)S(1)} %copy-done.1), custom_call_target="tpu_custom_call" | custom-call | flops 1 | bytes 1 | tf_op jit(solution)/shard_map/local_part/pallas_call | solution.py:140
  49.6 3.4 %collective-permute-done.13.refs_1_ = bf16[128,1024]{1,0:T(8,128)(2,1)S(1)} collective-permute-done((bf16[128,1024]{1,0:T(8,128)(2,1)S(1)}, bf16[128,1024]{1,0:T(8,128)(2,1)S(1)}, u32[]{:S(2)}, u32[]{:S(2)}) %collective-permute-start.13) | collective-permute-done | bytes 262176 | tf_op jit(solution)/shard_map/ppermute | solution.py:36
  53.0 3.5 %collective-permute-done.15.refs_2_ = bf16[4,512,128]{2,1,0:T(8,128)(2,1)S(1)} collective-permute-done((bf16[4,512,128]{2,1,0:T(8,128)(2,1)S(1)}, bf16[4,512,128]{2,1,0:T(8,128)(2,1)S(1)}, u32[]{:S(2)}, u32[]{:S(2)}) %collective-permute-start.15) | collective-permute-done | bytes 524320 | tf_op jit(solution)/shard_map/ppermute | solution.py:36
  59.6 2.4 %collective-permute-start.27 = (bf16[2,512,128]{2,1,0:T(8,128)(2,1)S(1)}, bf16[2,512,128]{2,1,0:T(8,128)(2,1)S(1)}, u32[]{:S(2)}, u32[]{:S(2)}) collective-permute-start(bf16[2,512,128]{2,1,0:T(8,128)(2,1)S(1)} %pad_maximum_fusion.2), channel_id=1, source_target_pairs={{0,24},{1,25},{2,26},{3,27},{4,100},{5,101},{6,102},{7,103},{8,0},... | collective-permute-start | bytes 786440 | tf_op jit(solution)/shard_map/ppermute | solution.py:36
  67.5 2.3 %collective-permute-start.23 = (bf16[128,1024]{1,0:T(8,128)(2,1)S(1)}, bf16[128,1024]{1,0:T(8,128)(2,1)S(1)}, u32[]{:S(2)}, u32[]{:S(2)}) collective-permute-start(bf16[128,1024]{1,0:T(8,128)(2,1)S(1)} %project_other.7), channel_id=1, source_target_pairs={{0,3},{1,2},{2,1},{3,0},{4,7},{5,6},{6,5},{7,4},{8,11},{9,10},{10,... | collective-permute-start | bytes 786440 | tf_op jit(solution)/shard_map/ppermute | solution.py:36
  72.5 2.2 %collective-permute-start.21 = (bf16[128,1024]{1,0:T(8,128)(2,1)S(1)}, bf16[128,1024]{1,0:T(8,128)(2,1)S(1)}, u32[]{:S(2)}, u32[]{:S(2)}) collective-permute-start(bf16[128,1024]{1,0:T(8,128)(2,1)S(1)} %project_other.6), channel_id=1, source_target_pairs={{0,3},{1,2},{2,1},{3,0},{4,7},{5,6},{6,5},{7,4},{8,11},{9,10},{10,... | collective-permute-start | bytes 786440 | tf_op jit(solution)/shard_map/ppermute | solution.py:36
  74.9 3.1 %collective-permute-done.12.refs_1_ = bf16[256,1024]{1,0:T(8,128)(2,1)S(1)} collective-permute-done((bf16[256,1024]{1,0:T(8,128)(2,1)S(1)}, bf16[256,1024]{1,0:T(8,128)(2,1)S(1)}, u32[]{:S(2)}, u32[]{:S(2)}) %collective-permute-start.12) | collective-permute-done | bytes 524320 | tf_op jit(solution)/shard_map/ppermute | solution.py:36
  82.0 2.3 %collective-permute-start.34 = (bf16[256,1024]{1,0:T(8,128)(2,1)S(1)}, bf16[256,1024]{1,0:T(8,128)(2,1)S(1)}, u32[]{:S(2)}, u32[]{:S(2)}) collective-permute-start(bf16[256,1024]{1,0:T(8,128)(2,1)S(1)} %project_other.8), channel_id=1, source_target_pairs={{0,3},{1,2},{2,1},{3,0},{4,7},{5,6},{6,5},{7,4},{8,11},{9,10},{10,... | collective-permute-start | bytes 1572872 | tf_op jit(solution)/shard_map/ppermute | solution.py:36
  84.3 2.3 %local_part.7 = (f32[256,1024]{1,0:T(8,128)S(1)}, bf16[256,1024]{1,0:T(8,128)(2,1)S(1)}) custom-call(bf16[1024,1024]{1,0:T(8,128)(2,1)S(1)} %copy-done.2, bf16[1024,1024]{1,0:T(8,128)(2,1)S(1)} %get-tuple-element.74.feat_ref, bf16[1024,1024]{1,0:T(8,128)(2,1)S(1)} %copy-done.1), custom_call_target="tpu_custom_call" | custom-call | flops 1 | bytes 1 | tf_op jit(solution)/shard_map/local_part/pallas_call | solution.py:140
  91.1 4.6 %collective-permute-done.33.refs_1_ = bf16[128,1024]{1,0:T(8,128)(2,1)S(1)} collective-permute-done((bf16[128,1024]{1,0:T(8,128)(2,1)S(1)}, bf16[128,1024]{1,0:T(8,128)(2,1)S(1)}, u32[]{:S(2)}, u32[]{:S(2)}) %collective-permute-start.33) | collective-permute-done | bytes 262176 | tf_op jit(solution)/shard_map/ppermute | solution.py:36
  95.6 2.2 %collective-permute-start.26 = (bf16[256,1024]{1,0:T(8,128)(2,1)S(1)}, bf16[256,1024]{1,0:T(8,128)(2,1)S(1)}, u32[]{:S(2)}, u32[]{:S(2)}) collective-permute-start(bf16[256,1024]{1,0:T(8,128)(2,1)S(1)} %project_other.9), channel_id=1, source_target_pairs={{0,3},{1,2},{2,1},{3,0},{4,7},{5,6},{6,5},{7,4},{8,11},{9,10},{10,... | collective-permute-start | bytes 1572872 | tf_op jit(solution)/shard_map/ppermute | solution.py:36
  99.5 5.7 %collective-permute-done.31.refs_2_ = bf16[4,2,512,128]{3,2,1,0:T(8,128)(2,1)S(1)} collective-permute-done((bf16[4,2,512,128]{3,2,1,0:T(8,128)(2,1)S(1)}, bf16[4,2,512,128]{3,2,1,0:T(8,128)(2,1)S(1)}, u32[]{:S(2)}, u32[]{:S(2)}) %collective-permute-start.31) | collective-permute-done | bytes 1048608 | tf_op jit(solution)/shard_map/ppermute | solution.py:36
  109.7 2.2 %collective-permute-start.36 = (bf16[128,1024]{1,0:T(8,128)(2,1)S(1)}, bf16[128,1024]{1,0:T(8,128)(2,1)S(1)}, u32[]{:S(2)}, u32[]{:S(2)}) collective-permute-start(bf16[128,1024]{1,0:T(8,128)(2,1)S(1)} %project_other.10), channel_id=1, source_target_pairs={{0,3},{1,2},{2,1},{3,0},{4,7},{5,6},{6,5},{7,4},{8,11},{9,10},{10,... | collective-permute-start | bytes 786440 | tf_op jit(solution)/shard_map/ppermute | solution.py:36
  111.9 2.0 %project_own.8.refs_4_ = bf16[1024,1024]{1,0:T(8,128)(2,1)} custom-call(bf16[256,1024]{1,0:T(8,128)(2,1)S(1)} %norm_part.8.refs_0_, bf16[256,1024]{1,0:T(8,128)(2,1)S(1)} %collective-permute-done.12.refs_1_, bf16[2,1024,1024]{2,1,0:T(8,128)(2,1)S(1)} %assemble.3.refs_2_, ...), custom_call_target="tpu_custom_call", output_to_operand_aliasing={{}: (4, {})} | custom-call | flops 1 | bytes 1 | tf_op jit(solution)/shard_map/project_own/pallas_call | solution.py:275
  119.9 3.0 %collective-permute-done.35.refs_3_ = bf16[128,1024]{1,0:T(8,128)(2,1)S(1)} collective-permute-done((bf16[128,1024]{1,0:T(8,128)(2,1)S(1)}, bf16[128,1024]{1,0:T(8,128)(2,1)S(1)}, u32[]{:S(2)}, u32[]{:S(2)}) %collective-permute-start.35) | collective-permute-done | bytes 262176 | tf_op jit(solution)/shard_map/ppermute | solution.py:36
  (94 shorter events, 54.7 us)
Async XLA Ops:
  1.0 10.9 %collective-permute-start = (bf16[512,128]{1,0:T(8,128)(2,1)S(1)}, bf16[512,128]{1,0:T(8,128)(2,1)S(1)}, u32[]{:S(2)}, u32[]{:S(2)}) collective-permute-start(bf16[512,128]{1,0:T(8,128)(2,1)S(1)} %get-tuple-element.134), channel_id=1, source_target_pairs={{0,0},{1,32},{2,35},{3,3},{4,4},{5,36},{6,39},{7,7},{8,8},{9,40},{... | collective-permute-start | bytes 393224 | tf_op jit(solution)/shard_map/ppermute | solution.py:36
  1.7 10.2 %collective-permute-start.1 = (bf16[512,128]{1,0:T(8,128)(2,1)S(1)}, bf16[512,128]{1,0:T(8,128)(2,1)S(1)}, u32[]{:S(2)}, u32[]{:S(2)}) collective-permute-start(bf16[512,128]{1,0:T(8,128)(2,1)S(1)} %get-tuple-element.133), channel_id=1, source_target_pairs={{0,96},{1,64},{2,67},{3,99},{4,100},{5,68},{6,71},{7,103},{8,104},... | collective-permute-start | bytes 393224 | tf_op jit(solution)/shard_map/ppermute | solution.py:36
  25.7 7.8 %collective-permute-start.5 = (bf16[4,128,128]{2,1,0:T(8,128)(2,1)S(1)}, bf16[4,128,128]{2,1,0:T(8,128)(2,1)S(1)}, u32[]{:S(2)}, u32[]{:S(2)}) collective-permute-start(bf16[4,128,128]{2,1,0:T(8,128)(2,1)S(1)} %get-tuple-element.84), channel_id=1, source_target_pairs={{0,32},{1,33},{2,34},{3,35},{4,36},{5,37},{6,38},{7,39},{8,40},{9,... | collective-permute-start | bytes 393224 | tf_op jit(solution)/shard_map/ppermute | solution.py:36
  34.2 7.9 %collective-permute-start.7 = (bf16[4,128,128]{2,1,0:T(8,128)(2,1)S(1)}, bf16[4,128,128]{2,1,0:T(8,128)(2,1)S(1)}, u32[]{:S(2)}, u32[]{:S(2)}) collective-permute-start(bf16[4,128,128]{2,1,0:T(8,128)(2,1)S(1)} %get-tuple-element.91), channel_id=1, source_target_pairs={{0,96},{1,97},{2,98},{3,99},{4,100},{5,101},{6,102},{7,103},{8,104... | collective-permute-start | bytes 393224 | tf_op jit(solution)/shard_map/ppermute | solution.py:36
  38.3 14.7 %collective-permute-start.14 = (bf16[4,512,128]{2,1,0:T(8,128)(2,1)S(1)}, bf16[4,512,128]{2,1,0:T(8,128)(2,1)S(1)}, u32[]{:S(2)}, u32[]{:S(2)}) collective-permute-start(bf16[4,512,128]{2,1,0:T(8,128)(2,1)S(1)} %pad_maximum_fusion.1.refs_0_), channel_id=1, source_target_pairs={{0,96},{1,97},{2,98},{3,99},{4,28},{5,29},{6,30},{7,31},{8,104},{9... | collective-permute-start | bytes 1572872 | tf_op jit(solution)/shard_map/ppermute | solution.py:36
  40.5 16.0 %collective-permute-start.15 = (bf16[4,512,128]{2,1,0:T(8,128)(2,1)S(1)}, bf16[4,512,128]{2,1,0:T(8,128)(2,1)S(1)}, u32[]{:S(2)}, u32[]{:S(2)}) collective-permute-start(bf16[4,512,128]{2,1,0:T(8,128)(2,1)S(1)} %pad_maximum_fusion.1.refs_0_), channel_id=1, source_target_pairs={{0,32},{1,33},{2,34},{3,35},{4,12},{5,13},{6,14},{7,15},{8,40},{9,... | collective-permute-start | bytes 1572872 | tf_op jit(solution)/shard_map/ppermute | solution.py:36
  40.5 16.0 %collective-permute-start.16 = (bf16[4,512,128]{2,1,0:T(8,128)(2,1)S(1)}, bf16[4,512,128]{2,1,0:T(8,128)(2,1)S(1)}, u32[]{:S(2)}, u32[]{:S(2)}) collective-permute-start(bf16[4,512,128]{2,1,0:T(8,128)(2,1)S(1)} %pad_maximum_fusion.1.refs_0_), channel_id=1, source_target_pairs={{0,64},{1,65},{2,66},{3,67},{4,20},{5,21},{6,22},{7,23},{8,72},{9,... | collective-permute-start | bytes 1572872 | tf_op jit(solution)/shard_map/ppermute | solution.py:36
  44.1 8.9 %collective-permute-start.13 = (bf16[128,1024]{1,0:T(8,128)(2,1)S(1)}, bf16[128,1024]{1,0:T(8,128)(2,1)S(1)}, u32[]{:S(2)}, u32[]{:S(2)}) collective-permute-start(bf16[128,1024]{1,0:T(8,128)(2,1)S(1)} %norm_part.6.refs_0_), channel_id=1, source_target_pairs={{0,1},{1,0},{2,3},{3,2},{4,5},{5,4},{6,7},{7,6},{8,9},{9,8},{10,11... | collective-permute-start | bytes 786440 | tf_op jit(solution)/shard_map/ppermute | solution.py:36
  57.6 9.2 %collective-permute-start.22 = (bf16[128,1024]{1,0:T(8,128)(2,1)S(1)}, bf16[128,1024]{1,0:T(8,128)(2,1)S(1)}, u32[]{:S(2)}, u32[]{:S(2)}) collective-permute-start(bf16[128,1024]{1,0:T(8,128)(2,1)S(1)} %norm_part.7.refs_0_), channel_id=1, source_target_pairs={{0,1},{1,0},{2,3},{3,2},{4,5},{5,4},{6,7},{7,6},{8,9},{9,8},{10,11... | collective-permute-start | bytes 786440 | tf_op jit(solution)/shard_map/ppermute | solution.py:36
  58.5 19.5 %collective-permute-start.12 = (bf16[256,1024]{1,0:T(8,128)(2,1)S(1)}, bf16[256,1024]{1,0:T(8,128)(2,1)S(1)}, u32[]{:S(2)}, u32[]{:S(2)}) collective-permute-start(bf16[256,1024]{1,0:T(8,128)(2,1)S(1)} %norm_part.8.refs_0_), channel_id=1, source_target_pairs={{0,1},{1,0},{2,3},{3,2},{4,5},{5,4},{6,7},{7,6},{8,9},{9,8},{10,11... | collective-permute-start | bytes 1572872 | tf_op jit(solution)/shard_map/ppermute | solution.py:36
  59.6 12.2 %collective-permute-start.27 = (bf16[2,512,128]{2,1,0:T(8,128)(2,1)S(1)}, bf16[2,512,128]{2,1,0:T(8,128)(2,1)S(1)}, u32[]{:S(2)}, u32[]{:S(2)}) collective-permute-start(bf16[2,512,128]{2,1,0:T(8,128)(2,1)S(1)} %pad_maximum_fusion.2), channel_id=1, source_target_pairs={{0,24},{1,25},{2,26},{3,27},{4,100},{5,101},{6,102},{7,103},{8,0},... | collective-permute-start | bytes 786440 | tf_op jit(solution)/shard_map/ppermute | solution.py:36
  62.1 10.4 %collective-permute-start.28 = (bf16[2,512,128]{2,1,0:T(8,128)(2,1)S(1)}, bf16[2,512,128]{2,1,0:T(8,128)(2,1)S(1)}, u32[]{:S(2)}, u32[]{:S(2)}) collective-permute-start(bf16[2,512,128]{2,1,0:T(8,128)(2,1)S(1)} %pad_maximum_fusion.2), channel_id=1, source_target_pairs={{0,8},{1,9},{2,10},{3,11},{4,36},{5,37},{6,38},{7,39},{8,16},{9,17... | collective-permute-start | bytes 786440 | tf_op jit(solution)/shard_map/ppermute | solution.py:36
  62.1 12.6 %collective-permute-start.29 = (bf16[2,512,128]{2,1,0:T(8,128)(2,1)S(1)}, bf16[2,512,128]{2,1,0:T(8,128)(2,1)S(1)}, u32[]{:S(2)}, u32[]{:S(2)}) collective-permute-start(bf16[2,512,128]{2,1,0:T(8,128)(2,1)S(1)} %pad_maximum_fusion.2), channel_id=1, source_target_pairs={{0,16},{1,17},{2,18},{3,19},{4,68},{5,69},{6,70},{7,71},{8,24},{9,... | collective-permute-start | bytes 786440 | tf_op jit(solution)/shard_map/ppermute | solution.py:36
  67.5 10.5 %collective-permute-start.23 = (bf16[128,1024]{1,0:T(8,128)(2,1)S(1)}, bf16[128,1024]{1,0:T(8,128)(2,1)S(1)}, u32[]{:S(2)}, u32[]{:S(2)}) collective-permute-start(bf16[128,1024]{1,0:T(8,128)(2,1)S(1)} %project_other.7), channel_id=1, source_target_pairs={{0,3},{1,2},{2,1},{3,0},{4,7},{5,6},{6,5},{7,4},{8,11},{9,10},{10,... | collective-permute-start | bytes 786440 | tf_op jit(solution)/shard_map/ppermute | solution.py:36
  71.8 16.5 %collective-permute-start.25 = (bf16[256,1024]{1,0:T(8,128)(2,1)S(1)}, bf16[256,1024]{1,0:T(8,128)(2,1)S(1)}, u32[]{:S(2)}, u32[]{:S(2)}) collective-permute-start(bf16[256,1024]{1,0:T(8,128)(2,1)S(1)} %norm_part.9.refs_0_), channel_id=1, source_target_pairs={{0,1},{1,0},{2,3},{3,2},{4,5},{5,4},{6,7},{7,6},{8,9},{9,8},{10,11... | collective-permute-start | bytes 1572872 | tf_op jit(solution)/shard_map/ppermute | solution.py:36
  72.5 8.3 %collective-permute-start.21 = (bf16[128,1024]{1,0:T(8,128)(2,1)S(1)}, bf16[128,1024]{1,0:T(8,128)(2,1)S(1)}, u32[]{:S(2)}, u32[]{:S(2)}) collective-permute-start(bf16[128,1024]{1,0:T(8,128)(2,1)S(1)} %project_other.6), channel_id=1, source_target_pairs={{0,3},{1,2},{2,1},{3,0},{4,7},{5,6},{6,5},{7,4},{8,11},{9,10},{10,... | collective-permute-start | bytes 786440 | tf_op jit(solution)/shard_map/ppermute | solution.py:36
  74.8 24.7 %collective-permute-start.30 = (bf16[4,2,512,128]{3,2,1,0:T(8,128)(2,1)S(1)}, bf16[4,2,512,128]{3,2,1,0:T(8,128)(2,1)S(1)}, u32[]{:S(2)}, u32[]{:S(2)}) collective-permute-start(bf16[4,2,512,128]{3,2,1,0:T(8,128)(2,1)S(1)} %pad_maximum_fusion.refs_0_), channel_id=1, source_target_pairs={{0,96},{1,97},{2,98},{3,99},{4,28},{5,29},{6,30},{7,31},{8,104},{9... | collective-permute-start | bytes 3145736 | tf_op jit(solution)/shard_map/ppermute | solution.py:36
  78.0 27.2 %collective-permute-start.31 = (bf16[4,2,512,128]{3,2,1,0:T(8,128)(2,1)S(1)}, bf16[4,2,512,128]{3,2,1,0:T(8,128)(2,1)S(1)}, u32[]{:S(2)}, u32[]{:S(2)}) collective-permute-start(bf16[4,2,512,128]{3,2,1,0:T(8,128)(2,1)S(1)} %pad_maximum_fusion.refs_0_), channel_id=1, source_target_pairs={{0,32},{1,33},{2,34},{3,35},{4,12},{5,13},{6,14},{7,15},{8,40},{9,... | collective-permute-start | bytes 3145736 | tf_op jit(solution)/shard_map/ppermute | solution.py:36
  78.0 27.2 %collective-permute-start.32 = (bf16[4,2,512,128]{3,2,1,0:T(8,128)(2,1)S(1)}, bf16[4,2,512,128]{3,2,1,0:T(8,128)(2,1)S(1)}, u32[]{:S(2)}, u32[]{:S(2)}) collective-permute-start(bf16[4,2,512,128]{3,2,1,0:T(8,128)(2,1)S(1)} %pad_maximum_fusion.refs_0_), channel_id=1, source_target_pairs={{0,64},{1,65},{2,66},{3,67},{4,20},{5,21},{6,22},{7,23},{8,72},{9,... | collective-permute-start | bytes 3145736 | tf_op jit(solution)/shard_map/ppermute | solution.py:36
  82.0 15.8 %collective-permute-start.34 = (bf16[256,1024]{1,0:T(8,128)(2,1)S(1)}, bf16[256,1024]{1,0:T(8,128)(2,1)S(1)}, u32[]{:S(2)}, u32[]{:S(2)}) collective-permute-start(bf16[256,1024]{1,0:T(8,128)(2,1)S(1)} %project_other.8), channel_id=1, source_target_pairs={{0,3},{1,2},{2,1},{3,0},{4,7},{5,6},{6,5},{7,4},{8,11},{9,10},{10,... | collective-permute-start | bytes 1572872 | tf_op jit(solution)/shard_map/ppermute | solution.py:36
  95.6 18.3 %collective-permute-start.26 = (bf16[256,1024]{1,0:T(8,128)(2,1)S(1)}, bf16[256,1024]{1,0:T(8,128)(2,1)S(1)}, u32[]{:S(2)}, u32[]{:S(2)}) collective-permute-start(bf16[256,1024]{1,0:T(8,128)(2,1)S(1)} %project_other.9), channel_id=1, source_target_pairs={{0,3},{1,2},{2,1},{3,0},{4,7},{5,6},{6,5},{7,4},{8,11},{9,10},{10,... | collective-permute-start | bytes 1572872 | tf_op jit(solution)/shard_map/ppermute | solution.py:36
  97.8 16.1 %collective-permute-start.24 = (bf16[128,1024]{1,0:T(8,128)(2,1)S(1)}, bf16[128,1024]{1,0:T(8,128)(2,1)S(1)}, u32[]{:S(2)}, u32[]{:S(2)}) collective-permute-start(bf16[128,1024]{1,0:T(8,128)(2,1)S(1)} %norm_part.11.refs_0_), channel_id=1, source_target_pairs={{0,1},{1,0},{2,3},{3,2},{4,5},{5,4},{6,7},{7,6},{8,9},{9,8},{10,11... | collective-permute-start | bytes 786440 | tf_op jit(solution)/shard_map/ppermute | solution.py:36
  109.7 8.8 %collective-permute-start.36 = (bf16[128,1024]{1,0:T(8,128)(2,1)S(1)}, bf16[128,1024]{1,0:T(8,128)(2,1)S(1)}, u32[]{:S(2)}, u32[]{:S(2)}) collective-permute-start(bf16[128,1024]{1,0:T(8,128)(2,1)S(1)} %project_other.10), channel_id=1, source_target_pairs={{0,3},{1,2},{2,1},{3,0},{4,7},{5,6},{6,5},{7,4},{8,11},{9,10},{10,... | collective-permute-start | bytes 786440 | tf_op jit(solution)/shard_map/ppermute | solution.py:36
  114.7 8.2 %collective-permute-start.35 = (bf16[128,1024]{1,0:T(8,128)(2,1)S(1)}, bf16[128,1024]{1,0:T(8,128)(2,1)S(1)}, u32[]{:S(2)}, u32[]{:S(2)}) collective-permute-start(bf16[128,1024]{1,0:T(8,128)(2,1)S(1)} %project_other.11), channel_id=1, source_target_pairs={{0,3},{1,2},{2,1},{3,0},{4,7},{5,6},{6,5},{7,4},{8,11},{9,10},{10,... | collective-permute-start | bytes 786440 | tf_op jit(solution)/shard_map/ppermute | solution.py:36
  (17 other events, 79.6 us)
where the time goes:
time: 125 us; the launch traced here: 124 us
  starting transfers between devices  48.2 us (39%)
  waiting for transfers between devices  38.8 us (31%)
  Pallas kernels  32.6 us (26%)
  local copies, waits for them, and re-layouts  4.17 us (3%)
    ppermute x37, starting transfers between devices, send(): return lax.ppermute(array, AXES, route(target))  48.2 us
    ppermute x37, waiting for transfers between devices, send(): return lax.ppermute(array, AXES, route(target))  38.8 us
    pallas_call x12, Pallas kernels, project(): pl.pallas_call(body, grid=(1,), in_specs=specs, out_specs=pl.BlockSpec((r...  15.1 us
    pallas_call x4, Pallas kernels, local_part(): pl.pallas_call(local_kernel, grid=(features // width,), in_specs=[rows, s...  7.76 us
    pallas_call x2, Pallas kernels, assemble(): pl.pallas_call(functools.partial(assemble_kernel, home, blocks), in_specs...  3.23 us
    unnamed x8, local copies, waits for them, and re-layouts  3.19 us
    pallas_call x1, Pallas kernels, states(): pl.pallas_call(state_kernel, in_specs=[pl.BlockSpec(memory_space=pltpu.HB...  2.83 us
  transfers between devices with their start and end apart: 37, of which 19 were waited for; matrix products, arithmetic and copies ran while one was open for 0% of the time, Pallas kernels for 25%

commit v1 on v0

--- a/solution.py
+++ b/solution.py
@@ -14,7 +14,7 @@
 NZ, NX, NC, NY = 4, 4, 2, 4
 OFFSETS = (0, 1, -1, 2)
 QROWS = 256
-CHUNKS = ((0, 128), (128, 128), (256, 256), (512, 256), (768, 128), (896, 128))
+CHUNKS = ((0, 128), (128, 128), (256, 256), (512, 256), (768, 256))
 VMEM_LIMIT = 10 * 1024 * 1024
 COST = pl.CostEstimate(flops=1, bytes_accessed=1, transcendentals=0)
 
@@ -400,22 +400,15 @@
 def on_device(queries, keys, values, out_weight):
     tokens = queries.shape[0]
 
-    ready, parts = spread_weight(out_weight)
-    key_feat, total, first = states(after(keys, ready), values)
+    key_feat, total, first = states(keys, values)
+    _, parts = spread_weight(after(out_weight, total))
     heads = total.shape[0]
     half = jax.ShapeDtypeStruct((heads // 2, HEAD_DIM, HEAD_DIM), jnp.bfloat16)
     wide_half = jax.ShapeDtypeStruct(half.shape, jnp.float32)
 
-    total = after(total, *parts)
     peer = send(total, other_core)
-    item = jax.ShapeDtypeStruct(parts[0].shape, parts[0].dtype)
-    own_item, other_item = small(
-        item_kernel, [item, item], *after(tuple(parts), total), name="weight_items"
-    )
-
     wide, chip = small(chip_kernel, [wide_half, half], total, peer, name="chip_sum")
     other_chip = send(chip, lambda z, x, c, y: (z, x ^ 1, c, y))
-    line = first_moves(after(other_item, chip))
     local = [local_part(after(queries, chip), key_feat, values, 0)]
     wide, chip, earlier = small(
         functools.partial(step_kernel, 1, 1),
@@ -425,6 +418,12 @@
         name="step_x",
     )
     other_chip = send(chip, lambda z, x, c, y: (z, 3 - x, c, y))
+    item = jax.ShapeDtypeStruct(parts[0].shape, parts[0].dtype)
+    own_item, other_item = small(
+        item_kernel, [item, item], *after(tuple(parts), chip), name="weight_items"
+    )
+    line = first_moves(other_item)
+    other_chip = after(other_chip, other_item)
     wide, chip, earlier = small(
         functools.partial(step_kernel, 1, 2),
         [wide_half, half, wide_half],
@@ -433,9 +432,7 @@
         other_chip,
         name="step_x2",
     )
-    own_pair = jnp.stack([own_item, send(after(own_item, chip), other_core)])
     other_chip = send(chip, lambda z, x, c, y: (z ^ 1, x, c, y))
-    other_chip = after(other_chip, own_pair)
     wide, chip, earlier = small(
         functools.partial(step_kernel, 0, 1),
         [wide_half, half, wide_half],
@@ -484,26 +481,31 @@
     def reply(index):
         received.append(send(partial[index], lambda z, x, c, y: (z, x, c, 3 - y)))
 
+    received = []
+
+    def reply(index):
+        received.append(send(partial[index], lambda z, x, c, y: (z, x, c, 3 - y)))
+
     norm(0)
     norm(1, normed[0])
     norm(2, normed[1])
-    own_line = first_moves(after(own_pair, normed[0]))
-    lines = list(after(tuple(lines), peers[0], normed[2]))
-    lines += [send(piece, other_core) for piece in lines]
-    weight = assemble(1, LINE_BLOCKS, *lines)
+    norm(3, normed[2])
+    norm(4, normed[3])
+    lines = list(after(tuple(lines), peers[0], peers[1], normed[4]))
+    swapped = [send(piece, other_core) for piece in lines]
+    weight = assemble(1, LINE_BLOCKS, *lines, *swapped)
     other(0)
     reply(0)
     peers[1] = after(peers[1], partial[0])
     other(1)
     reply(1)
-    own_lines = second_moves(jnp.stack(after(tuple(own_line), partial[1])))
-    norm(3, partial[1])
-    peers[2] = after(peers[2], received[0], received[1], normed[3])
+    own_pair = jnp.stack([own_item, send(after(own_item, partial[1]), other_core)])
+    own_line = first_moves(own_pair)
+    peers[2] = after(peers[2], received[0], normed[4])
     other(2)
     reply(2)
-    norm(4, partial[2])
-    norm(5, normed[4])
-    peers[3] = after(peers[3], normed[5])
+    own_lines = second_moves(jnp.stack(after(tuple(own_line), partial[2], received[1])))
+    peers[3] = after(peers[3], partial[2], received[1])
     other(3)
     reply(3)
     peers[4] = after(peers[4], received[2], partial[3])
@@ -511,20 +513,9 @@
     reply(4)
     own_weight = assemble(0, PAIR_BLOCKS, *after(tuple(own_lines), partial[4]))
     out = None
-
-    def own(index, *done):
-        row = CHUNKS[index][0]
-        back = after(received[index], *done) if done else received[index]
-        return project(normed[index], peers[index], own_weight, back, row, tokens, out)
-
-    for index in range(3):
-        out = own(index)
-    peers[5] = after(peers[5], received[3], out)
-    other(5)
-    reply(5)
-    out = own(3, partial[5])
-    out = own(4)
-    return own(5)
+    for (row, _), mine, peer, back in zip(CHUNKS, normed, peers, received):
+        out = project(mine, peer, own_weight, back, row, tokens, out)
+    return out
 
 
 def solution(mesh):

time: 125 us -> 121 us (0.968)
  waiting for transfers between devices: 38.8 us -> 37.2 us
    ppermute x37 -> x35, waiting for transfers between devices: 38.8 us -> 37.2 us  [send(): return lax.ppermute(array, AXES, route(target))]
    pallas_call x12 -> x10, Pallas kernels: 15.1 us -> 14.1 us  [project(): pl.pallas_call(body, grid=(1,), in_specs=specs, out_specs=pl.BlockSpec((r...]
    ppermute x37 -> x35, starting transfers between devices: 48.2 us -> 48.7 us  [send(): return lax.ppermute(array, AXES, route(target))]
    unnamed x8 -> x10, local copies, waits for them, and re-layouts: 3.19 us -> 3.19 us
  transfers between devices with their start and end apart: 37 -> 35, of which waited for: 19 -> 17; matrix products, arithmetic and copies ran while one was open for 0% -> 0% of each run, Pallas kernels for 25% -> 22%
where the time goes in v1:
time: 121 us
  starting transfers between devices  48.7 us (40%)
  waiting for transfers between devices  37.2 us (31%)
  Pallas kernels  31.4 us (26%)
  local copies, waits for them, and re-layouts  3.21 us (3%)
    ppermute x35, starting transfers between devices, send(): return lax.ppermute(array, AXES, route(target))  48.7 us
    ppermute x35, waiting for transfers between devices, send(): return lax.ppermute(array, AXES, route(target))  37.2 us
    pallas_call x10, Pallas kernels, project(): pl.pallas_call(body, grid=(1,), in_specs=specs, out_specs=pl.BlockSpec((r...  14.1 us
    pallas_call x4, Pallas kernels, local_part(): pl.pallas_call(local_kernel, grid=(features // width,), in_specs=[rows, s...  7.79 us
    pallas_call x2, Pallas kernels, assemble(): pl.pallas_call(functools.partial(assemble_kernel, home, blocks), in_specs...  3.23 us
    unnamed x10, local copies, waits for them, and re-layouts  3.19 us
    pallas_call x1, Pallas kernels, states(): pl.pallas_call(state_kernel, in_specs=[pl.BlockSpec(memory_space=pltpu.HB...  2.82 us
  transfers between devices with their start and end apart: 35, of which 17 were waited for; matrix products, arithmetic and copies ran while one was open for 0% of the time, Pallas kernels for 22%

profile of v1, /device:TPU:0, one launch (start us, length us, event | category | flops | bytes accessed | tf_op | source)
XLA Modules:
  0.0 121.0 jit_solution(10611839588256413336)
XLA Ops:
  3.2 2.8 %states.1 = (bf16[1024,1024]{1,0:T(8,128)(2,1)S(1)}, bf16[8,128,128]{2,1,0:T(8,128)(2,1)S(1)}, f32[8,128,128]{2,1,0:T(8,128)S(1)}) custom-call(bf16[1024,1024]{1,0:T(8,128)(2,1)S(1)} %copy-done.3, bf16[1024,1024]{1,0:T(8,128)(2,1)S(1)} %copy-done), custom_call_target="tpu_custom_call" | custom-call | flops 1 | bytes 1 | tf_op jit(solution)/shard_map/states/pallas_call | solution.py:88
  7.7 1.7 %collective-permute-start.1 = (bf16[4,128,128]{2,1,0:T(8,128)(2,1)S(1)}, bf16[4,128,128]{2,1,0:T(8,128)(2,1)S(1)}, u32[]{:S(2)}, u32[]{:S(2)}) collective-permute-start(bf16[4,128,128]{2,1,0:T(8,128)(2,1)S(1)} %get-tuple-element.64), channel_id=1, source_target_pairs={{0,8},{1,9},{2,10},{3,11},{4,12},{5,13},{6,14},{7,15},{8,0},{9,1},... | collective-permute-start | bytes 393224 | tf_op jit(solution)/shard_map/ppermute | solution.py:36
  9.4 4.1 %collective-permute-start.4 = (bf16[512,128]{1,0:T(8,128)(2,1)S(1)}, bf16[512,128]{1,0:T(8,128)(2,1)S(1)}, u32[]{:S(2)}, u32[]{:S(2)}) collective-permute-start(bf16[512,128]{1,0:T(8,128)(2,1)S(1)} %get-tuple-element.121), channel_id=1, source_target_pairs={{0,96},{1,64},{2,67},{3,99},{4,100},{5,68},{6,71},{7,103},{8,104},... | collective-permute-start | bytes 393224 | tf_op jit(solution)/shard_map/ppermute | solution.py:36
  15.8 2.2 %collective-permute-start.2 = (bf16[4,128,128]{2,1,0:T(8,128)(2,1)S(1)}, bf16[4,128,128]{2,1,0:T(8,128)(2,1)S(1)}, u32[]{:S(2)}, u32[]{:S(2)}) collective-permute-start(bf16[4,128,128]{2,1,0:T(8,128)(2,1)S(1)} %get-tuple-element.73), channel_id=1, source_target_pairs={{0,24},{1,25},{2,26},{3,27},{4,28},{5,29},{6,30},{7,31},{8,16},{9,... | collective-permute-start | bytes 393224 | tf_op jit(solution)/shard_map/ppermute | solution.py:36
  18.1 4.0 %collective-permute-done.2.refs_2_ = bf16[4,128,128]{2,1,0:T(8,128)(2,1)S(1)} collective-permute-done((bf16[4,128,128]{2,1,0:T(8,128)(2,1)S(1)}, bf16[4,128,128]{2,1,0:T(8,128)(2,1)S(1)}, u32[]{:S(2)}, u32[]{:S(2)}) %collective-permute-start.2) | collective-permute-done | bytes 131104 | tf_op jit(solution)/shard_map/ppermute | solution.py:36
  22.1 4.1 %collective-permute-start.5 = (bf16[4,128,128]{2,1,0:T(8,128)(2,1)S(1)}, bf16[4,128,128]{2,1,0:T(8,128)(2,1)S(1)}, u32[]{:S(2)}, u32[]{:S(2)}) collective-permute-start(bf16[4,128,128]{2,1,0:T(8,128)(2,1)S(1)} %get-tuple-element.81), channel_id=1, source_target_pairs={{0,32},{1,33},{2,34},{3,35},{4,36},{5,37},{6,38},{7,39},{8,40},{9,... | collective-permute-start | bytes 393224 | tf_op jit(solution)/shard_map/ppermute | solution.py:36
  29.2 1.8 %collective-permute-start.7 = (bf16[512,128]{1,0:T(8,128)(2,1)S(1)}, bf16[512,128]{1,0:T(8,128)(2,1)S(1)}, u32[]{:S(2)}, u32[]{:S(2)}) collective-permute-start(bf16[512,128]{1,0:T(8,128)(2,1)S(1)} %get-tuple-element.84), channel_id=1, source_target_pairs={{0,24},{1,25},{2,26},{3,27},{4,100},{5,101},{6,102},{7,103},{8,0},... | collective-permute-start | bytes 393224 | tf_op jit(solution)/shard_map/ppermute | solution.py:36
  36.0 2.8 %collective-permute-start.14 = (bf16[4,512,128]{2,1,0:T(8,128)(2,1)S(1)}, bf16[4,512,128]{2,1,0:T(8,128)(2,1)S(1)}, u32[]{:S(2)}, u32[]{:S(2)}) collective-permute-start(bf16[4,512,128]{2,1,0:T(8,128)(2,1)S(1)} %pad_maximum_fusion.1.refs_0_), channel_id=1, source_target_pairs={{0,96},{1,97},{2,98},{3,99},{4,28},{5,29},{6,30},{7,31},{8,104},{9... | collective-permute-start | bytes 1572872 | tf_op jit(solution)/shard_map/ppermute | solution.py:36
  43.3 2.3 %local_part.5 = (f32[256,1024]{1,0:T(8,128)S(1)}, bf16[256,1024]{1,0:T(8,128)(2,1)S(1)}) custom-call(bf16[1024,1024]{1,0:T(8,128)(2,1)S(1)} %copy-done.2, bf16[1024,1024]{1,0:T(8,128)(2,1)S(1)} %get-tuple-element.66.feat_ref, bf16[1024,1024]{1,0:T(8,128)(2,1)S(1)} %copy-done.1), custom_call_target="tpu_custom_call" | custom-call | flops 1 | bytes 1 | tf_op jit(solution)/shard_map/local_part/pallas_call | solution.py:140
  48.2 2.3 %local_part.7 = (f32[256,1024]{1,0:T(8,128)S(1)}, bf16[256,1024]{1,0:T(8,128)(2,1)S(1)}) custom-call(bf16[1024,1024]{1,0:T(8,128)(2,1)S(1)} %copy-done.2, bf16[1024,1024]{1,0:T(8,128)(2,1)S(1)} %get-tuple-element.66.feat_ref, bf16[1024,1024]{1,0:T(8,128)(2,1)S(1)} %copy-done.1), custom_call_target="tpu_custom_call" | custom-call | flops 1 | bytes 1 | tf_op jit(solution)/shard_map/local_part/pallas_call | solution.py:140
  51.1 4.1 %collective-permute-done.13.refs_1_ = bf16[128,1024]{1,0:T(8,128)(2,1)S(1)} collective-permute-done((bf16[128,1024]{1,0:T(8,128)(2,1)S(1)}, bf16[128,1024]{1,0:T(8,128)(2,1)S(1)}, u32[]{:S(2)}, u32[]{:S(2)}) %collective-permute-start.13) | collective-permute-done | bytes 262176 | tf_op jit(solution)/shard_map/ppermute | solution.py:36
  61.8 3.1 %collective-permute-start.22 = (bf16[128,1024]{1,0:T(8,128)(2,1)S(1)}, bf16[128,1024]{1,0:T(8,128)(2,1)S(1)}, u32[]{:S(2)}, u32[]{:S(2)}) collective-permute-start(bf16[128,1024]{1,0:T(8,128)(2,1)S(1)} %project_other.5), channel_id=1, source_target_pairs={{0,3},{1,2},{2,1},{3,0},{4,7},{5,6},{6,5},{7,4},{8,11},{9,10},{10,... | collective-permute-start | bytes 786440 | tf_op jit(solution)/shard_map/ppermute | solution.py:36
  68.7 2.4 %collective-permute-done.12.refs_1_ = bf16[256,1024]{1,0:T(8,128)(2,1)S(1)} collective-permute-done((bf16[256,1024]{1,0:T(8,128)(2,1)S(1)}, bf16[256,1024]{1,0:T(8,128)(2,1)S(1)}, u32[]{:S(2)}, u32[]{:S(2)}) %collective-permute-start.12) | collective-permute-done | bytes 524320 | tf_op jit(solution)/shard_map/ppermute | solution.py:36
  72.2 2.1 %collective-permute-start.27 = (bf16[2,512,128]{2,1,0:T(8,128)(2,1)S(1)}, bf16[2,512,128]{2,1,0:T(8,128)(2,1)S(1)}, u32[]{:S(2)}, u32[]{:S(2)}) collective-permute-start(bf16[2,512,128]{2,1,0:T(8,128)(2,1)S(1)} %pad_maximum_fusion.2), channel_id=1, source_target_pairs={{0,24},{1,25},{2,26},{3,27},{4,100},{5,101},{6,102},{7,103},{8,0},... | collective-permute-start | bytes 786440 | tf_op jit(solution)/shard_map/ppermute | solution.py:36
  81.2 2.4 %collective-permute-start.30 = (bf16[4,2,512,128]{3,2,1,0:T(8,128)(2,1)S(1)}, bf16[4,2,512,128]{3,2,1,0:T(8,128)(2,1)S(1)}, u32[]{:S(2)}, u32[]{:S(2)}) collective-permute-start(bf16[4,2,512,128]{3,2,1,0:T(8,128)(2,1)S(1)} %pad_maximum_fusion.refs_0_), channel_id=1, source_target_pairs={{0,96},{1,97},{2,98},{3,99},{4,28},{5,29},{6,30},{7,31},{8,104},{9... | collective-permute-start | bytes 3145736 | tf_op jit(solution)/shard_map/ppermute | solution.py:36
  84.3 2.3 %collective-permute-start.23 = (bf16[256,1024]{1,0:T(8,128)(2,1)S(1)}, bf16[256,1024]{1,0:T(8,128)(2,1)S(1)}, u32[]{:S(2)}, u32[]{:S(2)}) collective-permute-start(bf16[256,1024]{1,0:T(8,128)(2,1)S(1)} %project_other.6), channel_id=1, source_target_pairs={{0,3},{1,2},{2,1},{3,0},{4,7},{5,6},{6,5},{7,4},{8,11},{9,10},{10,... | collective-permute-start | bytes 1572872 | tf_op jit(solution)/shard_map/ppermute | solution.py:36
  87.9 7.2 %collective-permute-done.11.refs_1_ = bf16[256,1024]{1,0:T(8,128)(2,1)S(1)} collective-permute-done((bf16[256,1024]{1,0:T(8,128)(2,1)S(1)}, bf16[256,1024]{1,0:T(8,128)(2,1)S(1)}, u32[]{:S(2)}, u32[]{:S(2)}) %collective-permute-start.11) | collective-permute-done | bytes 524320 | tf_op jit(solution)/shard_map/ppermute | solution.py:36
  95.1 2.2 %collective-permute-start.34 = (bf16[256,1024]{1,0:T(8,128)(2,1)S(1)}, bf16[256,1024]{1,0:T(8,128)(2,1)S(1)}, u32[]{:S(2)}, u32[]{:S(2)}) collective-permute-start(bf16[256,1024]{1,0:T(8,128)(2,1)S(1)} %project_other.8), channel_id=1, source_target_pairs={{0,3},{1,2},{2,1},{3,0},{4,7},{5,6},{6,5},{7,4},{8,11},{9,10},{10,... | collective-permute-start | bytes 1572872 | tf_op jit(solution)/shard_map/ppermute | solution.py:36
  98.6 3.4 %collective-permute-start.33 = (bf16[256,1024]{1,0:T(8,128)(2,1)S(1)}, bf16[256,1024]{1,0:T(8,128)(2,1)S(1)}, u32[]{:S(2)}, u32[]{:S(2)}) collective-permute-start(bf16[256,1024]{1,0:T(8,128)(2,1)S(1)} %project_other.9), channel_id=1, source_target_pairs={{0,3},{1,2},{2,1},{3,0},{4,7},{5,6},{6,5},{7,4},{8,11},{9,10},{10,... | collective-permute-start | bytes 1572872 | tf_op jit(solution)/shard_map/ppermute | solution.py:36
  102.0 4.4 %collective-permute-done.31.refs_2_ = bf16[4,2,512,128]{3,2,1,0:T(8,128)(2,1)S(1)} collective-permute-done((bf16[4,2,512,128]{3,2,1,0:T(8,128)(2,1)S(1)}, bf16[4,2,512,128]{3,2,1,0:T(8,128)(2,1)S(1)}, u32[]{:S(2)}, u32[]{:S(2)}) %collective-permute-start.31) | collective-permute-done | bytes 1048608 | tf_op jit(solution)/shard_map/ppermute | solution.py:36
  110.9 2.0 %project_own.7.refs_4_ = bf16[1024,1024]{1,0:T(8,128)(2,1)} custom-call(bf16[256,1024]{1,0:T(8,128)(2,1)S(1)} %norm_part.7.refs_0_, bf16[256,1024]{1,0:T(8,128)(2,1)S(1)} %collective-permute-done.12.refs_1_, bf16[2,1024,1024]{2,1,0:T(8,128)(2,1)S(1)} %assemble.3.refs_2_, ...), custom_call_target="tpu_custom_call", output_to_operand_aliasing={{}: (4, {})} | custom-call | flops 1 | bytes 1 | tf_op jit(solution)/shard_map/project_own/pallas_call | solution.py:275
  112.9 2.0 %project_own.8.refs_4_ = bf16[1024,1024]{1,0:T(8,128)(2,1)} custom-call(bf16[256,1024]{1,0:T(8,128)(2,1)S(1)} %norm_part.8.refs_0_, bf16[256,1024]{1,0:T(8,128)(2,1)S(1)} %collective-permute-done.24.refs_1_, bf16[2,1024,1024]{2,1,0:T(8,128)(2,1)S(1)} %assemble.3.refs_2_, ...), custom_call_target="tpu_custom_call", output_to_operand_aliasing={{}: (4, {})} | custom-call | flops 1 | bytes 1 | tf_op jit(solution)/shard_map/project_own/pallas_call | solution.py:275
  115.0 4.0 %collective-permute-done.33.refs_3_ = bf16[256,1024]{1,0:T(8,128)(2,1)S(1)} collective-permute-done((bf16[256,1024]{1,0:T(8,128)(2,1)S(1)}, bf16[256,1024]{1,0:T(8,128)(2,1)S(1)}, u32[]{:S(2)}, u32[]{:S(2)}) %collective-permute-start.33) | collective-permute-done | bytes 524320 | tf_op jit(solution)/shard_map/ppermute | solution.py:36
  119.0 2.0 %project_own.9 = bf16[1024,1024]{1,0:T(8,128)(2,1)} custom-call(bf16[256,1024]{1,0:T(8,128)(2,1)S(1)} %norm_part.9.refs_0_, bf16[256,1024]{1,0:T(8,128)(2,1)S(1)} %collective-permute-done.11.refs_1_, bf16[2,1024,1024]{2,1,0:T(8,128)(2,1)S(1)} %assemble.3.refs_2_, ...), custom_call_target="tpu_custom_call", output_to_operand_aliasing={{}: (4, {})} | custom-call | flops 1 | bytes 1 | tf_op jit(solution)/shard_map/project_own/pallas_call | solution.py:275
  (89 shorter events, 48.8 us)
Async XLA Ops:
  7.7 8.0 %collective-permute-start.1 = (bf16[4,128,128]{2,1,0:T(8,128)(2,1)S(1)}, bf16[4,128,128]{2,1,0:T(8,128)(2,1)S(1)}, u32[]{:S(2)}, u32[]{:S(2)}) collective-permute-start(bf16[4,128,128]{2,1,0:T(8,128)(2,1)S(1)} %get-tuple-element.64), channel_id=1, source_target_pairs={{0,8},{1,9},{2,10},{3,11},{4,12},{5,13},{6,14},{7,15},{8,0},{9,1},... | collective-permute-start | bytes 393224 | tf_op jit(solution)/shard_map/ppermute | solution.py:36
  9.4 8.6 %collective-permute-start.4 = (bf16[512,128]{1,0:T(8,128)(2,1)S(1)}, bf16[512,128]{1,0:T(8,128)(2,1)S(1)}, u32[]{:S(2)}, u32[]{:S(2)}) collective-permute-start(bf16[512,128]{1,0:T(8,128)(2,1)S(1)} %get-tuple-element.121), channel_id=1, source_target_pairs={{0,96},{1,64},{2,67},{3,99},{4,100},{5,68},{6,71},{7,103},{8,104},... | collective-permute-start | bytes 393224 | tf_op jit(solution)/shard_map/ppermute | solution.py:36
  22.1 8.8 %collective-permute-start.5 = (bf16[4,128,128]{2,1,0:T(8,128)(2,1)S(1)}, bf16[4,128,128]{2,1,0:T(8,128)(2,1)S(1)}, u32[]{:S(2)}, u32[]{:S(2)}) collective-permute-start(bf16[4,128,128]{2,1,0:T(8,128)(2,1)S(1)} %get-tuple-element.81), channel_id=1, source_target_pairs={{0,32},{1,33},{2,34},{3,35},{4,36},{5,37},{6,38},{7,39},{8,40},{9,... | collective-permute-start | bytes 393224 | tf_op jit(solution)/shard_map/ppermute | solution.py:36
  26.2 6.5 %collective-permute-start.9 = (bf16[512,128]{1,0:T(8,128)(2,1)S(1)}, bf16[512,128]{1,0:T(8,128)(2,1)S(1)}, u32[]{:S(2)}, u32[]{:S(2)}) collective-permute-start(bf16[512,128]{1,0:T(8,128)(2,1)S(1)} %get-tuple-element.84), channel_id=1, source_target_pairs={{0,16},{1,17},{2,18},{3,19},{4,68},{5,69},{6,70},{7,71},{8,24},{9,... | collective-permute-start | bytes 393224 | tf_op jit(solution)/shard_map/ppermute | solution.py:36
  31.7 7.1 %collective-permute-start.6 = (bf16[4,128,128]{2,1,0:T(8,128)(2,1)S(1)}, bf16[4,128,128]{2,1,0:T(8,128)(2,1)S(1)}, u32[]{:S(2)}, u32[]{:S(2)}) collective-permute-start(bf16[4,128,128]{2,1,0:T(8,128)(2,1)S(1)} %get-tuple-element.83), channel_id=1, source_target_pairs={{0,96},{1,97},{2,98},{3,99},{4,100},{5,101},{6,102},{7,103},{8,104... | collective-permute-start | bytes 393224 | tf_op jit(solution)/shard_map/ppermute | solution.py:36
  34.2 16.9 %collective-permute-start.16 = (bf16[4,512,128]{2,1,0:T(8,128)(2,1)S(1)}, bf16[4,512,128]{2,1,0:T(8,128)(2,1)S(1)}, u32[]{:S(2)}, u32[]{:S(2)}) collective-permute-start(bf16[4,512,128]{2,1,0:T(8,128)(2,1)S(1)} %pad_maximum_fusion.1.refs_0_), channel_id=1, source_target_pairs={{0,64},{1,65},{2,66},{3,67},{4,20},{5,21},{6,22},{7,23},{8,72},{9,... | collective-permute-start | bytes 1572872 | tf_op jit(solution)/shard_map/ppermute | solution.py:36
  35.6 15.6 %collective-permute-start.15 = (bf16[4,512,128]{2,1,0:T(8,128)(2,1)S(1)}, bf16[4,512,128]{2,1,0:T(8,128)(2,1)S(1)}, u32[]{:S(2)}, u32[]{:S(2)}) collective-permute-start(bf16[4,512,128]{2,1,0:T(8,128)(2,1)S(1)} %pad_maximum_fusion.1.refs_0_), channel_id=1, source_target_pairs={{0,32},{1,33},{2,34},{3,35},{4,12},{5,13},{6,14},{7,15},{8,40},{9,... | collective-permute-start | bytes 1572872 | tf_op jit(solution)/shard_map/ppermute | solution.py:36
  36.0 15.1 %collective-permute-start.14 = (bf16[4,512,128]{2,1,0:T(8,128)(2,1)S(1)}, bf16[4,512,128]{2,1,0:T(8,128)(2,1)S(1)}, u32[]{:S(2)}, u32[]{:S(2)}) collective-permute-start(bf16[4,512,128]{2,1,0:T(8,128)(2,1)S(1)} %pad_maximum_fusion.1.refs_0_), channel_id=1, source_target_pairs={{0,96},{1,97},{2,98},{3,99},{4,28},{5,29},{6,30},{7,31},{8,104},{9... | collective-permute-start | bytes 1572872 | tf_op jit(solution)/shard_map/ppermute | solution.py:36
  41.2 9.9 %collective-permute-start.17 = (bf16[128,1024]{1,0:T(8,128)(2,1)S(1)}, bf16[128,1024]{1,0:T(8,128)(2,1)S(1)}, u32[]{:S(2)}, u32[]{:S(2)}) collective-permute-start(bf16[128,1024]{1,0:T(8,128)(2,1)S(1)} %norm_part.6.refs_0_), channel_id=1, source_target_pairs={{0,1},{1,0},{2,3},{3,2},{4,5},{5,4},{6,7},{7,6},{8,9},{9,8},{10,11... | collective-permute-start | bytes 786440 | tf_op jit(solution)/shard_map/ppermute | solution.py:36
  42.6 12.7 %collective-permute-start.13 = (bf16[128,1024]{1,0:T(8,128)(2,1)S(1)}, bf16[128,1024]{1,0:T(8,128)(2,1)S(1)}, u32[]{:S(2)}, u32[]{:S(2)}) collective-permute-start(bf16[128,1024]{1,0:T(8,128)(2,1)S(1)} %norm_part.5.refs_0_), channel_id=1, source_target_pairs={{0,1},{1,0},{2,3},{3,2},{4,5},{5,4},{6,7},{7,6},{8,9},{9,8},{10,11... | collective-permute-start | bytes 786440 | tf_op jit(solution)/shard_map/ppermute | solution.py:36
  56.3 14.8 %collective-permute-start.12 = (bf16[256,1024]{1,0:T(8,128)(2,1)S(1)}, bf16[256,1024]{1,0:T(8,128)(2,1)S(1)}, u32[]{:S(2)}, u32[]{:S(2)}) collective-permute-start(bf16[256,1024]{1,0:T(8,128)(2,1)S(1)} %norm_part.7.refs_0_), channel_id=1, source_target_pairs={{0,1},{1,0},{2,3},{3,2},{4,5},{5,4},{6,7},{7,6},{8,9},{9,8},{10,11... | collective-permute-start | bytes 1572872 | tf_op jit(solution)/shard_map/ppermute | solution.py:36
  61.8 10.4 %collective-permute-start.22 = (bf16[128,1024]{1,0:T(8,128)(2,1)S(1)}, bf16[128,1024]{1,0:T(8,128)(2,1)S(1)}, u32[]{:S(2)}, u32[]{:S(2)}) collective-permute-start(bf16[128,1024]{1,0:T(8,128)(2,1)S(1)} %project_other.5), channel_id=1, source_target_pairs={{0,3},{1,2},{2,1},{3,0},{4,7},{5,6},{6,5},{7,4},{8,11},{9,10},{10,... | collective-permute-start | bytes 786440 | tf_op jit(solution)/shard_map/ppermute | solution.py:36
  65.7 18.6 %collective-permute-start.24 = (bf16[256,1024]{1,0:T(8,128)(2,1)S(1)}, bf16[256,1024]{1,0:T(8,128)(2,1)S(1)}, u32[]{:S(2)}, u32[]{:S(2)}) collective-permute-start(bf16[256,1024]{1,0:T(8,128)(2,1)S(1)} %norm_part.8.refs_0_), channel_id=1, source_target_pairs={{0,1},{1,0},{2,3},{3,2},{4,5},{5,4},{6,7},{7,6},{8,9},{9,8},{10,11... | collective-permute-start | bytes 1572872 | tf_op jit(solution)/shard_map/ppermute | solution.py:36
  65.8 11.3 %collective-permute-start.25 = (bf16[128,1024]{1,0:T(8,128)(2,1)S(1)}, bf16[128,1024]{1,0:T(8,128)(2,1)S(1)}, u32[]{:S(2)}, u32[]{:S(2)}) collective-permute-start(bf16[128,1024]{1,0:T(8,128)(2,1)S(1)} %project_other.7), channel_id=1, source_target_pairs={{0,3},{1,2},{2,1},{3,0},{4,7},{5,6},{6,5},{7,4},{8,11},{9,10},{10,... | collective-permute-start | bytes 786440 | tf_op jit(solution)/shard_map/ppermute | solution.py:36
  67.1 10.0 %collective-permute-start.29 = (bf16[2,512,128]{2,1,0:T(8,128)(2,1)S(1)}, bf16[2,512,128]{2,1,0:T(8,128)(2,1)S(1)}, u32[]{:S(2)}, u32[]{:S(2)}) collective-permute-start(bf16[2,512,128]{2,1,0:T(8,128)(2,1)S(1)} %pad_maximum_fusion.2), channel_id=1, source_target_pairs={{0,16},{1,17},{2,18},{3,19},{4,68},{5,69},{6,70},{7,71},{8,24},{9,... | collective-permute-start | bytes 786440 | tf_op jit(solution)/shard_map/ppermute | solution.py:36
  71.1 7.6 %collective-permute-start.28 = (bf16[2,512,128]{2,1,0:T(8,128)(2,1)S(1)}, bf16[2,512,128]{2,1,0:T(8,128)(2,1)S(1)}, u32[]{:S(2)}, u32[]{:S(2)}) collective-permute-start(bf16[2,512,128]{2,1,0:T(8,128)(2,1)S(1)} %pad_maximum_fusion.2), channel_id=1, source_target_pairs={{0,8},{1,9},{2,10},{3,11},{4,36},{5,37},{6,38},{7,39},{8,16},{9,17... | collective-permute-start | bytes 786440 | tf_op jit(solution)/shard_map/ppermute | solution.py:36
  72.2 6.5 %collective-permute-start.27 = (bf16[2,512,128]{2,1,0:T(8,128)(2,1)S(1)}, bf16[2,512,128]{2,1,0:T(8,128)(2,1)S(1)}, u32[]{:S(2)}, u32[]{:S(2)}) collective-permute-start(bf16[2,512,128]{2,1,0:T(8,128)(2,1)S(1)} %pad_maximum_fusion.2), channel_id=1, source_target_pairs={{0,24},{1,25},{2,26},{3,27},{4,100},{5,101},{6,102},{7,103},{8,0},... | collective-permute-start | bytes 786440 | tf_op jit(solution)/shard_map/ppermute | solution.py:36
  78.8 23.2 %collective-permute-start.32 = (bf16[4,2,512,128]{3,2,1,0:T(8,128)(2,1)S(1)}, bf16[4,2,512,128]{3,2,1,0:T(8,128)(2,1)S(1)}, u32[]{:S(2)}, u32[]{:S(2)}) collective-permute-start(bf16[4,2,512,128]{3,2,1,0:T(8,128)(2,1)S(1)} %pad_maximum_fusion.refs_0_), channel_id=1, source_target_pairs={{0,64},{1,65},{2,66},{3,67},{4,20},{5,21},{6,22},{7,23},{8,72},{9,... | collective-permute-start | bytes 3145736 | tf_op jit(solution)/shard_map/ppermute | solution.py:36
  80.4 26.0 %collective-permute-start.31 = (bf16[4,2,512,128]{3,2,1,0:T(8,128)(2,1)S(1)}, bf16[4,2,512,128]{3,2,1,0:T(8,128)(2,1)S(1)}, u32[]{:S(2)}, u32[]{:S(2)}) collective-permute-start(bf16[4,2,512,128]{3,2,1,0:T(8,128)(2,1)S(1)} %pad_maximum_fusion.refs_0_), channel_id=1, source_target_pairs={{0,32},{1,33},{2,34},{3,35},{4,12},{5,13},{6,14},{7,15},{8,40},{9,... | collective-permute-start | bytes 3145736 | tf_op jit(solution)/shard_map/ppermute | solution.py:36
  81.2 25.2 %collective-permute-start.30 = (bf16[4,2,512,128]{3,2,1,0:T(8,128)(2,1)S(1)}, bf16[4,2,512,128]{3,2,1,0:T(8,128)(2,1)S(1)}, u32[]{:S(2)}, u32[]{:S(2)}) collective-permute-start(bf16[4,2,512,128]{3,2,1,0:T(8,128)(2,1)S(1)} %pad_maximum_fusion.refs_0_), channel_id=1, source_target_pairs={{0,96},{1,97},{2,98},{3,99},{4,28},{5,29},{6,30},{7,31},{8,104},{9... | collective-permute-start | bytes 3145736 | tf_op jit(solution)/shard_map/ppermute | solution.py:36
  83.6 11.5 %collective-permute-start.11 = (bf16[256,1024]{1,0:T(8,128)(2,1)S(1)}, bf16[256,1024]{1,0:T(8,128)(2,1)S(1)}, u32[]{:S(2)}, u32[]{:S(2)}) collective-permute-start(bf16[256,1024]{1,0:T(8,128)(2,1)S(1)} %norm_part.9.refs_0_), channel_id=1, source_target_pairs={{0,1},{1,0},{2,3},{3,2},{4,5},{5,4},{6,7},{7,6},{8,9},{9,8},{10,11... | collective-permute-start | bytes 1572872 | tf_op jit(solution)/shard_map/ppermute | solution.py:36
  84.3 13.0 %collective-permute-start.23 = (bf16[256,1024]{1,0:T(8,128)(2,1)S(1)}, bf16[256,1024]{1,0:T(8,128)(2,1)S(1)}, u32[]{:S(2)}, u32[]{:S(2)}) collective-permute-start(bf16[256,1024]{1,0:T(8,128)(2,1)S(1)} %project_other.6), channel_id=1, source_target_pairs={{0,3},{1,2},{2,1},{3,0},{4,7},{5,6},{6,5},{7,4},{8,11},{9,10},{10,... | collective-permute-start | bytes 1572872 | tf_op jit(solution)/shard_map/ppermute | solution.py:36
  95.1 17.8 %collective-permute-start.34 = (bf16[256,1024]{1,0:T(8,128)(2,1)S(1)}, bf16[256,1024]{1,0:T(8,128)(2,1)S(1)}, u32[]{:S(2)}, u32[]{:S(2)}) collective-permute-start(bf16[256,1024]{1,0:T(8,128)(2,1)S(1)} %project_other.8), channel_id=1, source_target_pairs={{0,3},{1,2},{2,1},{3,0},{4,7},{5,6},{6,5},{7,4},{8,11},{9,10},{10,... | collective-permute-start | bytes 1572872 | tf_op jit(solution)/shard_map/ppermute | solution.py:36
  98.6 20.4 %collective-permute-start.33 = (bf16[256,1024]{1,0:T(8,128)(2,1)S(1)}, bf16[256,1024]{1,0:T(8,128)(2,1)S(1)}, u32[]{:S(2)}, u32[]{:S(2)}) collective-permute-start(bf16[256,1024]{1,0:T(8,128)(2,1)S(1)} %project_other.9), channel_id=1, source_target_pairs={{0,3},{1,2},{2,1},{3,0},{4,7},{5,6},{6,5},{7,4},{8,11},{9,10},{10,... | collective-permute-start | bytes 1572872 | tf_op jit(solution)/shard_map/ppermute | solution.py:36
  (16 other events, 69.3 us)

commit v2 on v1

--- a/solution.py
+++ b/solution.py
@@ -245,43 +245,73 @@
     )(*pieces)
 
 
-def project_kernel(normed_ref, peer_ref, weight_ref, out_ref, *, received_ref=None):
+def product(normed_ref, peer_ref, weight_ref):
     total = jnp.dot(normed_ref[...], weight_ref[0], preferred_element_type=jnp.float32)
-    total += jnp.dot(peer_ref[...], weight_ref[1], preferred_element_type=jnp.float32)
-    if received_ref is not None:
-        total += received_ref[...].astype(jnp.float32)
-    out_ref[...] = total.astype(jnp.bfloat16)
-
-
-def project(normed, peer, weight, received=None, row=0, tokens=0, target=None):
+    return total + jnp.dot(peer_ref[...], weight_ref[1], preferred_element_type=jnp.float32)
+
+
+def other_kernel(normed_ref, peer_ref, weight_ref, *out_refs):
+    total = product(normed_ref, peer_ref, weight_ref).astype(jnp.bfloat16)
+    rows = out_refs[0].shape[0]
+    for index, out_ref in enumerate(out_refs):
+        out_ref[...] = total[index * rows : (index + 1) * rows]
+
+
+def project_other(normed, peer, weight, parts):
     rows, features = normed.shape
-    own = received is not None
-    chunk = pl.BlockSpec((rows, features), lambda i: (0, 0))
-    place = row // rows if own else 0
-    operands = [normed, peer, weight]
-    specs = [chunk, chunk, pl.BlockSpec(weight.shape, lambda i: (0, 0, 0))]
+    out = jax.ShapeDtypeStruct((rows // parts, features), jnp.bfloat16)
+    return pl.pallas_call(
+        other_kernel,
+        out_shape=[out] * parts,
+        compiler_params=params(),
+        cost_estimate=COST,
+        name="project_other",
+    )(normed, peer, weight)
+
+
+def own_kernel(parts, normed_refs, peer_refs, weight_ref, received_refs, out_ref):
+    row = 0
+    received_refs = list(received_refs)
+    for count, normed_ref, peer_ref in zip(parts, normed_refs, peer_refs):
+        total = product(normed_ref, peer_ref, weight_ref)
+        place = 0
+        for _ in range(count):
+            back_ref = received_refs.pop(0)
+            rows = back_ref.shape[0]
+            done = total[place : place + rows] + back_ref[...].astype(jnp.float32)
+            out_ref[row : row + rows] = done.astype(jnp.bfloat16)
+            place += rows
+            row += rows
+
+
+def project_own(normed, peers, weight, received, place, tokens, target):
+    features = weight.shape[-1]
+    rows = sum(chunk.shape[0] for chunk in normed)
+    parts = [len(group) for group in received]
+    flat = [part for group in received for part in group]
+    count = len(normed)
+    operands = [*normed, *peers, weight, *flat]
+    specs = [pl.BlockSpec(array.shape, lambda i, n=array.ndim: (0,) * n) for array in operands]
     aliases = {}
-    if own:
-        operands.append(received)
-        specs.append(chunk)
     if target is not None:
         aliases = {len(operands): 0}
         operands.append(target)
         specs.append(pl.BlockSpec(memory_space=pl.ANY))
 
     def body(*refs):
-        project_kernel(*refs[:3], refs[-1], received_ref=refs[3] if own else None)
+        back = refs[2 * count + 1 : 2 * count + 1 + len(flat)]
+        own_kernel(parts, refs[:count], refs[count : 2 * count], refs[2 * count], back, refs[-1])
 
     return pl.pallas_call(
         body,
         grid=(1,),
         in_specs=specs,
-        out_specs=pl.BlockSpec((rows, features), lambda i: (place, 0)),
-        out_shape=jax.ShapeDtypeStruct((tokens if own else rows, features), jnp.bfloat16),
+        out_specs=pl.BlockSpec((rows, features), lambda i: (place // rows, 0)),
+        out_shape=jax.ShapeDtypeStruct((tokens, features), jnp.bfloat16),
         input_output_aliases=aliases,
         compiler_params=params(),
         cost_estimate=COST,
-        name="project_own" if own else "project_other",
+        name="project_own",
     )(*operands)
 
 
@@ -361,6 +391,12 @@
 
 def first_moves(item):
     return [item] + [send(item, functools.partial(line_move, True, away)) for away in OFFSETS[1:]]
+
+
+def paced_moves(item, first):
+    near = [send(item, functools.partial(line_move, first, away)) for away in OFFSETS[1:3]]
+    far = send(after(item, *near), functools.partial(line_move, first, OFFSETS[3]))
+    return [item, *near, far]
 
 
 def second_moves(line):
@@ -456,7 +492,8 @@
         name="start_states",
     )
 
-    normed, peers, partial = [], [], []
+    normed, peers, partial, received = [], [], [], []
+    parts = (1, 1, 1, 1, 1)
 
     def norm(index, *done):
         place, rows = CHUNKS[index]
@@ -465,57 +502,38 @@
             local.append(local_part(after(queries, *done), key_feat, values, number))
         query_feat = after(local[number][1], *done) if done else local[number][1]
         normed.append(norm_part(local[number][0], query_feat, start, place, rows))
-        peers.append(send(normed[-1], lambda z, x, c, y: (z, x, c, y ^ 1)))
-
-    def other(index):
-        partial.append(project(normed[index], peers[index], weight))
-        return partial[-1]
-
-    received = []
-
-    def reply(index):
-        received.append(send(partial[index], lambda z, x, c, y: (z, x, c, 3 - y)))
-
-    received = []
-
-    def reply(index):
-        received.append(send(partial[index], lambda z, x, c, y: (z, x, c, 3 - y)))
-
-    received = []
-
-    def reply(index):
-        received.append(send(partial[index], lambda z, x, c, y: (z, x, c, 3 - y)))
+        ready = after(normed[-1], peers[1]) if index == 2 else normed[-1]
+        peers.append(send(ready, lambda z, x, c, y: (z, x, c, y ^ 1)))
+
+    def other(index, *done):
+        if done:
+            peers[index] = after(peers[index], *done)
+        partial.append(project_other(normed[index], peers[index], weight, parts[index]))
+        received.append(
+            [send(part, lambda z, x, c, y: (z, x, c, 3 - y)) for part in partial[index]]
+        )
 
     norm(0)
     norm(1, normed[0])
     norm(2, normed[1])
     norm(3, normed[2])
-    norm(4, normed[3])
-    lines = list(after(tuple(lines), peers[0], peers[1], normed[4]))
+    lines = list(after(tuple(lines), peers[0], normed[3]))
     swapped = [send(piece, other_core) for piece in lines]
     weight = assemble(1, LINE_BLOCKS, *lines, *swapped)
     other(0)
-    reply(0)
-    peers[1] = after(peers[1], partial[0])
-    other(1)
-    reply(1)
-    own_pair = jnp.stack([own_item, send(after(own_item, partial[1]), other_core)])
+    norm(4, partial[0][0])
+    other(1, normed[4])
+    own_pair = jnp.stack([own_item, send(after(own_item, partial[1][0]), other_core)])
     own_line = first_moves(own_pair)
-    peers[2] = after(peers[2], received[0], normed[4])
-    other(2)
-    reply(2)
-    own_lines = second_moves(jnp.stack(after(tuple(own_line), partial[2], received[1])))
-    peers[3] = after(peers[3], partial[2], received[1])
-    other(3)
-    reply(3)
-    peers[4] = after(peers[4], received[2], partial[3])
-    other(4)
-    reply(4)
-    own_weight = assemble(0, PAIR_BLOCKS, *after(tuple(own_lines), partial[4]))
-    out = None
-    for (row, _), mine, peer, back in zip(CHUNKS, normed, peers, received):
-        out = project(mine, peer, own_weight, back, row, tokens, out)
-    return out
+    other(2, received[0][0], normed[4])
+    own_lines = second_moves(jnp.stack(after(tuple(own_line), partial[2][0], received[1][0])))
+    other(3, partial[2][0], received[1][0], received[2][0])
+    other(4, partial[3][0])
+    own_weight = assemble(0, PAIR_BLOCKS, *after(tuple(own_lines), partial[4][0]))
+    out = project_own(normed[:4], peers[:4], own_weight, received[:4], 0, tokens, None)
+    return project_own(
+        normed[4:], peers[4:], own_weight, received[4:], CHUNKS[4][0], tokens, out
+    )
 
 
 def solution(mesh):

time: 121 us -> 118 us (0.975)
  Pallas kernels: 31.4 us -> 29.3 us
  starting transfers between devices: 48.7 us -> 47.2 us
    pallas_call x10 -> x7, Pallas kernels: 14.1 us -> 11.8 us  [the longest x2 6.61 us: project_own(): pl.pallas_call(body, grid=(1,), in_specs=specs, out_specs=pl.BlockSpec((r...]
    ppermute x35, starting transfers between devices: 48.7 us -> 47.2 us  [send(): return lax.ppermute(array, AXES, route(target))]
  transfers between devices with their start and end apart: 35 -> 35, of which waited for: 17 -> 14; matrix products, arithmetic and copies ran while one was open for 0% -> 0% of each run, Pallas kernels for 22% -> 21%
where the time goes in v2:
time: 118 us
  starting transfers between devices  47.2 us (40%)
  waiting for transfers between devices  37.5 us (32%)
  Pallas kernels  29.3 us (25%)
  local copies, waits for them, and re-layouts  3.21 us (3%)
    ppermute x35, starting transfers between devices, send(): return lax.ppermute(array, AXES, route(target))  47.2 us
    ppermute x35, waiting for transfers between devices, send(): return lax.ppermute(array, AXES, route(target))  37.5 us
    pallas_call x4, Pallas kernels, local_part(): pl.pallas_call(local_kernel, grid=(features // width,), in_specs=[rows, s...  7.77 us
    pallas_call x2, Pallas kernels, project_own(): pl.pallas_call(body, grid=(1,), in_specs=specs, out_specs=pl.BlockSpec((r...  6.61 us
    pallas_call x5, Pallas kernels, project_other(): pl.pallas_call(other_kernel, out_shape=[out] * parts, compiler_params=par...  5.18 us
    pallas_call x2, Pallas kernels, assemble(): pl.pallas_call(functools.partial(assemble_kernel, home, blocks), in_specs...  3.47 us
    unnamed x10, local copies, waits for them, and re-layouts  3.19 us
    pallas_call x1, Pallas kernels, states(): pl.pallas_call(state_kernel, in_specs=[pl.BlockSpec(memory_space=pltpu.HB...  2.82 us
  transfers between devices with their start and end apart: 35, of which 14 were waited for; matrix products, arithmetic and copies ran while one was open for 0% of the time, Pallas kernels for 21%

profile of v2, /device:TPU:0, one launch (start us, length us, event | category | flops | bytes accessed | tf_op | source)
XLA Modules:
  0.0 117.7 jit_solution(13174684748385652708)
XLA Ops:
  3.2 2.8 %states.1 = (bf16[1024,1024]{1,0:T(8,128)(2,1)S(1)}, bf16[8,128,128]{2,1,0:T(8,128)(2,1)S(1)}, f32[8,128,128]{2,1,0:T(8,128)S(1)}) custom-call(bf16[1024,1024]{1,0:T(8,128)(2,1)S(1)} %copy-done.3, bf16[1024,1024]{1,0:T(8,128)(2,1)S(1)} %copy-done), custom_call_target="tpu_custom_call" | custom-call | flops 1 | bytes 1 | tf_op jit(solution)/shard_map/states/pallas_call | solution.py:88
  9.4 4.1 %collective-permute-start.4 = (bf16[512,128]{1,0:T(8,128)(2,1)S(1)}, bf16[512,128]{1,0:T(8,128)(2,1)S(1)}, u32[]{:S(2)}, u32[]{:S(2)}) collective-permute-start(bf16[512,128]{1,0:T(8,128)(2,1)S(1)} %get-tuple-element.123), channel_id=1, source_target_pairs={{0,96},{1,64},{2,67},{3,99},{4,100},{5,68},{6,71},{7,103},{8,104},... | collective-permute-start | bytes 393224 | tf_op jit(solution)/shard_map/ppermute | solution.py:36
  15.8 2.2 %collective-permute-start.2 = (bf16[4,128,128]{2,1,0:T(8,128)(2,1)S(1)}, bf16[4,128,128]{2,1,0:T(8,128)(2,1)S(1)}, u32[]{:S(2)}, u32[]{:S(2)}) collective-permute-start(bf16[4,128,128]{2,1,0:T(8,128)(2,1)S(1)} %get-tuple-element.74), channel_id=1, source_target_pairs={{0,24},{1,25},{2,26},{3,27},{4,28},{5,29},{6,30},{7,31},{8,16},{9,... | collective-permute-start | bytes 393224 | tf_op jit(solution)/shard_map/ppermute | solution.py:36
  18.1 4.0 %collective-permute-done.2.refs_2_ = bf16[4,128,128]{2,1,0:T(8,128)(2,1)S(1)} collective-permute-done((bf16[4,128,128]{2,1,0:T(8,128)(2,1)S(1)}, bf16[4,128,128]{2,1,0:T(8,128)(2,1)S(1)}, u32[]{:S(2)}, u32[]{:S(2)}) %collective-permute-start.2) | collective-permute-done | bytes 131104 | tf_op jit(solution)/shard_map/ppermute | solution.py:36
  22.1 4.1 %collective-permute-start.5 = (bf16[4,128,128]{2,1,0:T(8,128)(2,1)S(1)}, bf16[4,128,128]{2,1,0:T(8,128)(2,1)S(1)}, u32[]{:S(2)}, u32[]{:S(2)}) collective-permute-start(bf16[4,128,128]{2,1,0:T(8,128)(2,1)S(1)} %get-tuple-element.82), channel_id=1, source_target_pairs={{0,32},{1,33},{2,34},{3,35},{4,36},{5,37},{6,38},{7,39},{8,40},{9,... | collective-permute-start | bytes 393224 | tf_op jit(solution)/shard_map/ppermute | solution.py:36
  29.2 1.8 %collective-permute-start.7 = (bf16[512,128]{1,0:T(8,128)(2,1)S(1)}, bf16[512,128]{1,0:T(8,128)(2,1)S(1)}, u32[]{:S(2)}, u32[]{:S(2)}) collective-permute-start(bf16[512,128]{1,0:T(8,128)(2,1)S(1)} %get-tuple-element.85), channel_id=1, source_target_pairs={{0,24},{1,25},{2,26},{3,27},{4,100},{5,101},{6,102},{7,103},{8,0},... | collective-permute-start | bytes 393224 | tf_op jit(solution)/shard_map/ppermute | solution.py:36
  36.0 2.8 %collective-permute-start.12 = (bf16[4,512,128]{2,1,0:T(8,128)(2,1)S(1)}, bf16[4,512,128]{2,1,0:T(8,128)(2,1)S(1)}, u32[]{:S(2)}, u32[]{:S(2)}) collective-permute-start(bf16[4,512,128]{2,1,0:T(8,128)(2,1)S(1)} %pad_maximum_fusion.1.refs_0_), channel_id=1, source_target_pairs={{0,96},{1,97},{2,98},{3,99},{4,28},{5,29},{6,30},{7,31},{8,104},{9... | collective-permute-start | bytes 1572872 | tf_op jit(solution)/shard_map/ppermute | solution.py:36
  43.4 2.3 %local_part.5 = (f32[256,1024]{1,0:T(8,128)S(1)}, bf16[256,1024]{1,0:T(8,128)(2,1)S(1)}) custom-call(bf16[1024,1024]{1,0:T(8,128)(2,1)S(1)} %copy-done.2, bf16[1024,1024]{1,0:T(8,128)(2,1)S(1)} %get-tuple-element.67.feat_ref, bf16[1024,1024]{1,0:T(8,128)(2,1)S(1)} %copy-done.1), custom_call_target="tpu_custom_call" | custom-call | flops 1 | bytes 1 | tf_op jit(solution)/shard_map/local_part/pallas_call | solution.py:140
  48.3 2.3 %collective-permute-done.13.refs_2_ = bf16[4,512,128]{2,1,0:T(8,128)(2,1)S(1)} collective-permute-done((bf16[4,512,128]{2,1,0:T(8,128)(2,1)S(1)}, bf16[4,512,128]{2,1,0:T(8,128)(2,1)S(1)}, u32[]{:S(2)}, u32[]{:S(2)}) %collective-permute-start.13) | collective-permute-done | bytes 524320 | tf_op jit(solution)/shard_map/ppermute | solution.py:36
  51.6 3.3 %collective-permute-done.21.peer_ref.refs_5_ = bf16[128,1024]{1,0:T(8,128)(2,1)S(1)} collective-permute-done((bf16[128,1024]{1,0:T(8,128)(2,1)S(1)}, bf16[128,1024]{1,0:T(8,128)(2,1)S(1)}, u32[]{:S(2)}, u32[]{:S(2)}) %collective-permute-start.21) | collective-permute-done | bytes 262176 | tf_op jit(solution)/shard_map/ppermute | solution.py:36
  56.2 1.9 %assemble.2.weight_ref = bf16[2,1024,1024]{2,1,0:T(8,128)(2,1)S(1)} custom-call(bf16[4,512,128]{2,1,0:T(8,128)(2,1)S(1)} %pad_maximum_fusion.1.refs_0_, bf16[4,512,128]{2,1,0:T(8,128)(2,1)S(1)} %collective-permute-done.12.refs_1_, bf16[4,512,128]{2,1,0:T(8,128)(2,1)S(1)} %collective-permute-done.13.refs_2_, ...), custom_call_target="tpu_custom_call" | custom-call | flops 1 | bytes 1 | tf_op jit(solution)/shard_map/assemble/pallas_call | solution.py:236
  58.8 2.3 %collective-permute-start.23 = (bf16[128,1024]{1,0:T(8,128)(2,1)S(1)}, bf16[128,1024]{1,0:T(8,128)(2,1)S(1)}, u32[]{:S(2)}, u32[]{:S(2)}) collective-permute-start(bf16[128,1024]{1,0:T(8,128)(2,1)S(1)} %project_other.5), channel_id=1, source_target_pairs={{0,3},{1,2},{2,1},{3,0},{4,7},{5,6},{6,5},{7,4},{8,11},{9,10},{10,... | collective-permute-start | bytes 786440 | tf_op jit(solution)/shard_map/ppermute | solution.py:36
  61.0 2.3 %local_part.7 = (f32[256,1024]{1,0:T(8,128)S(1)}, bf16[256,1024]{1,0:T(8,128)(2,1)S(1)}) custom-call(bf16[1024,1024]{1,0:T(8,128)(2,1)S(1)} %copy-done.2, bf16[1024,1024]{1,0:T(8,128)(2,1)S(1)} %get-tuple-element.67.feat_ref, bf16[1024,1024]{1,0:T(8,128)(2,1)S(1)} %copy-done.1), custom_call_target="tpu_custom_call" | custom-call | flops 1 | bytes 1 | tf_op jit(solution)/shard_map/local_part/pallas_call | solution.py:140
  69.5 1.9 %collective-permute-start.27 = (bf16[2,512,128]{2,1,0:T(8,128)(2,1)S(1)}, bf16[2,512,128]{2,1,0:T(8,128)(2,1)S(1)}, u32[]{:S(2)}, u32[]{:S(2)}) collective-permute-start(bf16[2,512,128]{2,1,0:T(8,128)(2,1)S(1)} %pad_maximum_fusion.2), channel_id=1, source_target_pairs={{0,24},{1,25},{2,26},{3,27},{4,100},{5,101},{6,102},{7,103},{8,0},... | collective-permute-start | bytes 786440 | tf_op jit(solution)/shard_map/ppermute | solution.py:36
  72.7 2.7 %collective-permute-done.24.refs_10_ = bf16[128,1024]{1,0:T(8,128)(2,1)S(1)} collective-permute-done((bf16[128,1024]{1,0:T(8,128)(2,1)S(1)}, bf16[128,1024]{1,0:T(8,128)(2,1)S(1)}, u32[]{:S(2)}, u32[]{:S(2)}) %collective-permute-start.24) | collective-permute-done | bytes 262176 | tf_op jit(solution)/shard_map/ppermute | solution.py:36
  75.3 2.0 %collective-permute-start.25 = (bf16[256,1024]{1,0:T(8,128)(2,1)S(1)}, bf16[256,1024]{1,0:T(8,128)(2,1)S(1)}, u32[]{:S(2)}, u32[]{:S(2)}) collective-permute-start(bf16[256,1024]{1,0:T(8,128)(2,1)S(1)} %project_other.6), channel_id=1, source_target_pairs={{0,3},{1,2},{2,1},{3,0},{4,7},{5,6},{6,5},{7,4},{8,11},{9,10},{10,... | collective-permute-start | bytes 1572872 | tf_op jit(solution)/shard_map/ppermute | solution.py:36
  79.8 2.3 %collective-permute-start.30 = (bf16[4,2,512,128]{3,2,1,0:T(8,128)(2,1)S(1)}, bf16[4,2,512,128]{3,2,1,0:T(8,128)(2,1)S(1)}, u32[]{:S(2)}, u32[]{:S(2)}) collective-permute-start(bf16[4,2,512,128]{3,2,1,0:T(8,128)(2,1)S(1)} %pad_maximum_fusion.refs_0_), channel_id=1, source_target_pairs={{0,96},{1,97},{2,98},{3,99},{4,28},{5,29},{6,30},{7,31},{8,104},{9... | collective-permute-start | bytes 3145736 | tf_op jit(solution)/shard_map/ppermute | solution.py:36
  82.8 6.9 %collective-permute-done.25.refs_11_ = bf16[256,1024]{1,0:T(8,128)(2,1)S(1)} collective-permute-done((bf16[256,1024]{1,0:T(8,128)(2,1)S(1)}, bf16[256,1024]{1,0:T(8,128)(2,1)S(1)}, u32[]{:S(2)}, u32[]{:S(2)}) %collective-permute-start.25) | collective-permute-done | bytes 524320 | tf_op jit(solution)/shard_map/ppermute | solution.py:36
  91.7 2.2 %collective-permute-done.19.peer_ref.refs_1_ = bf16[256,1024]{1,0:T(8,128)(2,1)S(1)} collective-permute-done((bf16[256,1024]{1,0:T(8,128)(2,1)S(1)}, bf16[256,1024]{1,0:T(8,128)(2,1)S(1)}, u32[]{:S(2)}, u32[]{:S(2)}) %collective-permute-start.19) | collective-permute-done | bytes 524320 | tf_op jit(solution)/shard_map/ppermute | solution.py:36
  95.1 2.9 %collective-permute-start.33 = (bf16[256,1024]{1,0:T(8,128)(2,1)S(1)}, bf16[256,1024]{1,0:T(8,128)(2,1)S(1)}, u32[]{:S(2)}, u32[]{:S(2)}) collective-permute-start(bf16[256,1024]{1,0:T(8,128)(2,1)S(1)} %project_other.9), channel_id=1, source_target_pairs={{0,3},{1,2},{2,1},{3,0},{4,7},{5,6},{6,5},{7,4},{8,11},{9,10},{10,... | collective-permute-start | bytes 1572872 | tf_op jit(solution)/shard_map/ppermute | solution.py:36
  98.0 7.1 %collective-permute-done.31.refs_2_ = bf16[4,2,512,128]{3,2,1,0:T(8,128)(2,1)S(1)} collective-permute-done((bf16[4,2,512,128]{3,2,1,0:T(8,128)(2,1)S(1)}, bf16[4,2,512,128]{3,2,1,0:T(8,128)(2,1)S(1)}, u32[]{:S(2)}, u32[]{:S(2)}) %collective-permute-start.31) | collective-permute-done | bytes 1048608 | tf_op jit(solution)/shard_map/ppermute | solution.py:36
  107.1 4.6 %project_own.2.refs_4_ = bf16[1024,1024]{1,0:T(8,128)(2,1)} custom-call(bf16[128,1024]{1,0:T(8,128)(2,1)S(1)} %norm_part.5.normed_ref.refs_0_, bf16[128,1024]{1,0:T(8,128)(2,1)S(1)} %norm_part.6.normed_ref.refs_1_, bf16[256,1024]{1,0:T(8,128)(2,1)S(1)} %norm_part.7.normed_ref.refs_2_, bf16[256,1024]{1,0:T(8,128)(2,1)S(1)} %norm_part.8.normed_ref.refs_3_, ...), custom_call_target="tpu_custom_call" | custom-call | flops 1 | bytes 1 | tf_op jit(solution)/shard_map/project_own/pallas_call | solution.py:305
  111.7 4.0 %collective-permute-done.33.refs_3_ = bf16[256,1024]{1,0:T(8,128)(2,1)S(1)} collective-permute-done((bf16[256,1024]{1,0:T(8,128)(2,1)S(1)}, bf16[256,1024]{1,0:T(8,128)(2,1)S(1)}, u32[]{:S(2)}, u32[]{:S(2)}) %collective-permute-start.33) | collective-permute-done | bytes 524320 | tf_op jit(solution)/shard_map/ppermute | solution.py:36
  115.7 2.0 %project_own.3 = bf16[1024,1024]{1,0:T(8,128)(2,1)} custom-call(bf16[256,1024]{1,0:T(8,128)(2,1)S(1)} %norm_part.9.normed_ref.refs_0_, bf16[256,1024]{1,0:T(8,128)(2,1)S(1)} %collective-permute-done.19.peer_ref.refs_1_, bf16[2,1024,1024]{2,1,0:T(8,128)(2,1)S(1)} %assemble.3.refs_8_.refs_2_, ...), custom_call_target="tpu_custom_call", output_to_operand_aliasing={{}: (4, {})} | custom-call | flops 1 | bytes 1 | tf_op jit(solution)/shard_map/project_own/pallas_call | solution.py:305
  (86 shorter events, 42.8 us)
Async XLA Ops:
  7.7 8.1 %collective-permute-start.1 = (bf16[4,128,128]{2,1,0:T(8,128)(2,1)S(1)}, bf16[4,128,128]{2,1,0:T(8,128)(2,1)S(1)}, u32[]{:S(2)}, u32[]{:S(2)}) collective-permute-start(bf16[4,128,128]{2,1,0:T(8,128)(2,1)S(1)} %get-tuple-element.65), channel_id=1, source_target_pairs={{0,8},{1,9},{2,10},{3,11},{4,12},{5,13},{6,14},{7,15},{8,0},{9,1},... | collective-permute-start | bytes 393224 | tf_op jit(solution)/shard_map/ppermute | solution.py:36
  9.4 8.6 %collective-permute-start.4 = (bf16[512,128]{1,0:T(8,128)(2,1)S(1)}, bf16[512,128]{1,0:T(8,128)(2,1)S(1)}, u32[]{:S(2)}, u32[]{:S(2)}) collective-permute-start(bf16[512,128]{1,0:T(8,128)(2,1)S(1)} %get-tuple-element.123), channel_id=1, source_target_pairs={{0,96},{1,64},{2,67},{3,99},{4,100},{5,68},{6,71},{7,103},{8,104},... | collective-permute-start | bytes 393224 | tf_op jit(solution)/shard_map/ppermute | solution.py:36
  22.1 8.8 %collective-permute-start.5 = (bf16[4,128,128]{2,1,0:T(8,128)(2,1)S(1)}, bf16[4,128,128]{2,1,0:T(8,128)(2,1)S(1)}, u32[]{:S(2)}, u32[]{:S(2)}) collective-permute-start(bf16[4,128,128]{2,1,0:T(8,128)(2,1)S(1)} %get-tuple-element.82), channel_id=1, source_target_pairs={{0,32},{1,33},{2,34},{3,35},{4,36},{5,37},{6,38},{7,39},{8,40},{9,... | collective-permute-start | bytes 393224 | tf_op jit(solution)/shard_map/ppermute | solution.py:36
  26.2 6.5 %collective-permute-start.9 = (bf16[512,128]{1,0:T(8,128)(2,1)S(1)}, bf16[512,128]{1,0:T(8,128)(2,1)S(1)}, u32[]{:S(2)}, u32[]{:S(2)}) collective-permute-start(bf16[512,128]{1,0:T(8,128)(2,1)S(1)} %get-tuple-element.85), channel_id=1, source_target_pairs={{0,16},{1,17},{2,18},{3,19},{4,68},{5,69},{6,70},{7,71},{8,24},{9,... | collective-permute-start | bytes 393224 | tf_op jit(solution)/shard_map/ppermute | solution.py:36
  31.7 7.1 %collective-permute-start.6 = (bf16[4,128,128]{2,1,0:T(8,128)(2,1)S(1)}, bf16[4,128,128]{2,1,0:T(8,128)(2,1)S(1)}, u32[]{:S(2)}, u32[]{:S(2)}) collective-permute-start(bf16[4,128,128]{2,1,0:T(8,128)(2,1)S(1)} %get-tuple-element.84), channel_id=1, source_target_pairs={{0,96},{1,97},{2,98},{3,99},{4,100},{5,101},{6,102},{7,103},{8,104... | collective-permute-start | bytes 393224 | tf_op jit(solution)/shard_map/ppermute | solution.py:36
  34.2 14.1 %collective-permute-start.14 = (bf16[4,512,128]{2,1,0:T(8,128)(2,1)S(1)}, bf16[4,512,128]{2,1,0:T(8,128)(2,1)S(1)}, u32[]{:S(2)}, u32[]{:S(2)}) collective-permute-start(bf16[4,512,128]{2,1,0:T(8,128)(2,1)S(1)} %pad_maximum_fusion.1.refs_0_), channel_id=1, source_target_pairs={{0,64},{1,65},{2,66},{3,67},{4,20},{5,21},{6,22},{7,23},{8,72},{9,... | collective-permute-start | bytes 1572872 | tf_op jit(solution)/shard_map/ppermute | solution.py:36
  35.6 15.0 %collective-permute-start.13 = (bf16[4,512,128]{2,1,0:T(8,128)(2,1)S(1)}, bf16[4,512,128]{2,1,0:T(8,128)(2,1)S(1)}, u32[]{:S(2)}, u32[]{:S(2)}) collective-permute-start(bf16[4,512,128]{2,1,0:T(8,128)(2,1)S(1)} %pad_maximum_fusion.1.refs_0_), channel_id=1, source_target_pairs={{0,32},{1,33},{2,34},{3,35},{4,12},{5,13},{6,14},{7,15},{8,40},{9,... | collective-permute-start | bytes 1572872 | tf_op jit(solution)/shard_map/ppermute | solution.py:36
  36.0 14.6 %collective-permute-start.12 = (bf16[4,512,128]{2,1,0:T(8,128)(2,1)S(1)}, bf16[4,512,128]{2,1,0:T(8,128)(2,1)S(1)}, u32[]{:S(2)}, u32[]{:S(2)}) collective-permute-start(bf16[4,512,128]{2,1,0:T(8,128)(2,1)S(1)} %pad_maximum_fusion.1.refs_0_), channel_id=1, source_target_pairs={{0,96},{1,97},{2,98},{3,99},{4,28},{5,29},{6,30},{7,31},{8,104},{9... | collective-permute-start | bytes 1572872 | tf_op jit(solution)/shard_map/ppermute | solution.py:36
  40.8 9.8 %collective-permute-start.11 = (bf16[128,1024]{1,0:T(8,128)(2,1)S(1)}, bf16[128,1024]{1,0:T(8,128)(2,1)S(1)}, u32[]{:S(2)}, u32[]{:S(2)}) collective-permute-start(bf16[128,1024]{1,0:T(8,128)(2,1)S(1)} %norm_part.5.normed_ref.refs_0_), channel_id=1, source_target_pairs={{0,1},{1,0},{2,3},{3,2},{4,5},{5,4},{6,7},{7,6},{8,9},{9,8},{10,11... | collective-permute-start | bytes 786440 | tf_op jit(solution)/shard_map/ppermute | solution.py:36
  42.5 12.3 %collective-permute-start.21 = (bf16[128,1024]{1,0:T(8,128)(2,1)S(1)}, bf16[128,1024]{1,0:T(8,128)(2,1)S(1)}, u32[]{:S(2)}, u32[]{:S(2)}) collective-permute-start(bf16[128,1024]{1,0:T(8,128)(2,1)S(1)} %norm_part.6.normed_ref.refs_1_), channel_id=1, source_target_pairs={{0,1},{1,0},{2,3},{3,2},{4,5},{5,4},{6,7},{7,6},{8,9},{9,8},{10,11... | collective-permute-start | bytes 786440 | tf_op jit(solution)/shard_map/ppermute | solution.py:36
  54.9 13.3 %collective-permute-start.22 = (bf16[256,1024]{1,0:T(8,128)(2,1)S(1)}, bf16[256,1024]{1,0:T(8,128)(2,1)S(1)}, u32[]{:S(2)}, u32[]{:S(2)}) collective-permute-start(bf16[256,1024]{1,0:T(8,128)(2,1)S(1)} %norm_part.7.normed_ref.refs_2_), channel_id=1, source_target_pairs={{0,1},{1,0},{2,3},{3,2},{4,5},{5,4},{6,7},{7,6},{8,9},{9,8},{10,11... | collective-permute-start | bytes 1572872 | tf_op jit(solution)/shard_map/ppermute | solution.py:36
  58.8 10.7 %collective-permute-start.23 = (bf16[128,1024]{1,0:T(8,128)(2,1)S(1)}, bf16[128,1024]{1,0:T(8,128)(2,1)S(1)}, u32[]{:S(2)}, u32[]{:S(2)}) collective-permute-start(bf16[128,1024]{1,0:T(8,128)(2,1)S(1)} %project_other.5), channel_id=1, source_target_pairs={{0,3},{1,2},{2,1},{3,0},{4,7},{5,6},{6,5},{7,4},{8,11},{9,10},{10,... | collective-permute-start | bytes 786440 | tf_op jit(solution)/shard_map/ppermute | solution.py:36
  64.7 17.3 %collective-permute-start.20 = (bf16[256,1024]{1,0:T(8,128)(2,1)S(1)}, bf16[256,1024]{1,0:T(8,128)(2,1)S(1)}, u32[]{:S(2)}, u32[]{:S(2)}) collective-permute-start(bf16[256,1024]{1,0:T(8,128)(2,1)S(1)} %norm_part.8.normed_ref.refs_3_), channel_id=1, source_target_pairs={{0,1},{1,0},{2,3},{3,2},{4,5},{5,4},{6,7},{7,6},{8,9},{9,8},{10,11... | collective-permute-start | bytes 1572872 | tf_op jit(solution)/shard_map/ppermute | solution.py:36
  65.8 9.6 %collective-permute-start.24 = (bf16[128,1024]{1,0:T(8,128)(2,1)S(1)}, bf16[128,1024]{1,0:T(8,128)(2,1)S(1)}, u32[]{:S(2)}, u32[]{:S(2)}) collective-permute-start(bf16[128,1024]{1,0:T(8,128)(2,1)S(1)} %project_other.7), channel_id=1, source_target_pairs={{0,3},{1,2},{2,1},{3,0},{4,7},{5,6},{6,5},{7,4},{8,11},{9,10},{10,... | collective-permute-start | bytes 786440 | tf_op jit(solution)/shard_map/ppermute | solution.py:36
  66.4 10.9 %collective-permute-start.29 = (bf16[2,512,128]{2,1,0:T(8,128)(2,1)S(1)}, bf16[2,512,128]{2,1,0:T(8,128)(2,1)S(1)}, u32[]{:S(2)}, u32[]{:S(2)}) collective-permute-start(bf16[2,512,128]{2,1,0:T(8,128)(2,1)S(1)} %pad_maximum_fusion.2), channel_id=1, source_target_pairs={{0,16},{1,17},{2,18},{3,19},{4,68},{5,69},{6,70},{7,71},{8,24},{9,... | collective-permute-start | bytes 786440 | tf_op jit(solution)/shard_map/ppermute | solution.py:36
  68.2 9.2 %collective-permute-start.28 = (bf16[2,512,128]{2,1,0:T(8,128)(2,1)S(1)}, bf16[2,512,128]{2,1,0:T(8,128)(2,1)S(1)}, u32[]{:S(2)}, u32[]{:S(2)}) collective-permute-start(bf16[2,512,128]{2,1,0:T(8,128)(2,1)S(1)} %pad_maximum_fusion.2), channel_id=1, source_target_pairs={{0,8},{1,9},{2,10},{3,11},{4,36},{5,37},{6,38},{7,39},{8,16},{9,17... | collective-permute-start | bytes 786440 | tf_op jit(solution)/shard_map/ppermute | solution.py:36
  69.5 7.8 %collective-permute-start.27 = (bf16[2,512,128]{2,1,0:T(8,128)(2,1)S(1)}, bf16[2,512,128]{2,1,0:T(8,128)(2,1)S(1)}, u32[]{:S(2)}, u32[]{:S(2)}) collective-permute-start(bf16[2,512,128]{2,1,0:T(8,128)(2,1)S(1)} %pad_maximum_fusion.2), channel_id=1, source_target_pairs={{0,24},{1,25},{2,26},{3,27},{4,100},{5,101},{6,102},{7,103},{8,0},... | collective-permute-start | bytes 786440 | tf_op jit(solution)/shard_map/ppermute | solution.py:36
  75.3 14.4 %collective-permute-start.25 = (bf16[256,1024]{1,0:T(8,128)(2,1)S(1)}, bf16[256,1024]{1,0:T(8,128)(2,1)S(1)}, u32[]{:S(2)}, u32[]{:S(2)}) collective-permute-start(bf16[256,1024]{1,0:T(8,128)(2,1)S(1)} %project_other.6), channel_id=1, source_target_pairs={{0,3},{1,2},{2,1},{3,0},{4,7},{5,6},{6,5},{7,4},{8,11},{9,10},{10,... | collective-permute-start | bytes 1572872 | tf_op jit(solution)/shard_map/ppermute | solution.py:36
  77.5 20.6 %collective-permute-start.32 = (bf16[4,2,512,128]{3,2,1,0:T(8,128)(2,1)S(1)}, bf16[4,2,512,128]{3,2,1,0:T(8,128)(2,1)S(1)}, u32[]{:S(2)}, u32[]{:S(2)}) collective-permute-start(bf16[4,2,512,128]{3,2,1,0:T(8,128)(2,1)S(1)} %pad_maximum_fusion.refs_0_), channel_id=1, source_target_pairs={{0,64},{1,65},{2,66},{3,67},{4,20},{5,21},{6,22},{7,23},{8,72},{9,... | collective-permute-start | bytes 3145736 | tf_op jit(solution)/shard_map/ppermute | solution.py:36
  78.8 26.3 %collective-permute-start.31 = (bf16[4,2,512,128]{3,2,1,0:T(8,128)(2,1)S(1)}, bf16[4,2,512,128]{3,2,1,0:T(8,128)(2,1)S(1)}, u32[]{:S(2)}, u32[]{:S(2)}) collective-permute-start(bf16[4,2,512,128]{3,2,1,0:T(8,128)(2,1)S(1)} %pad_maximum_fusion.refs_0_), channel_id=1, source_target_pairs={{0,32},{1,33},{2,34},{3,35},{4,12},{5,13},{6,14},{7,15},{8,40},{9,... | collective-permute-start | bytes 3145736 | tf_op jit(solution)/shard_map/ppermute | solution.py:36
  79.8 25.3 %collective-permute-start.30 = (bf16[4,2,512,128]{3,2,1,0:T(8,128)(2,1)S(1)}, bf16[4,2,512,128]{3,2,1,0:T(8,128)(2,1)S(1)}, u32[]{:S(2)}, u32[]{:S(2)}) collective-permute-start(bf16[4,2,512,128]{3,2,1,0:T(8,128)(2,1)S(1)} %pad_maximum_fusion.refs_0_), channel_id=1, source_target_pairs={{0,96},{1,97},{2,98},{3,99},{4,28},{5,29},{6,30},{7,31},{8,104},{9... | collective-permute-start | bytes 3145736 | tf_op jit(solution)/shard_map/ppermute | solution.py:36
  82.1 11.8 %collective-permute-start.19 = (bf16[256,1024]{1,0:T(8,128)(2,1)S(1)}, bf16[256,1024]{1,0:T(8,128)(2,1)S(1)}, u32[]{:S(2)}, u32[]{:S(2)}) collective-permute-start(bf16[256,1024]{1,0:T(8,128)(2,1)S(1)} %norm_part.9.normed_ref.refs_0_), channel_id=1, source_target_pairs={{0,1},{1,0},{2,3},{3,2},{4,5},{5,4},{6,7},{7,6},{8,9},{9,8},{10,11... | collective-permute-start | bytes 1572872 | tf_op jit(solution)/shard_map/ppermute | solution.py:36
  90.9 16.2 %collective-permute-start.34 = (bf16[256,1024]{1,0:T(8,128)(2,1)S(1)}, bf16[256,1024]{1,0:T(8,128)(2,1)S(1)}, u32[]{:S(2)}, u32[]{:S(2)}) collective-permute-start(bf16[256,1024]{1,0:T(8,128)(2,1)S(1)} %project_other.8), channel_id=1, source_target_pairs={{0,3},{1,2},{2,1},{3,0},{4,7},{5,6},{6,5},{7,4},{8,11},{9,10},{10,... | collective-permute-start | bytes 1572872 | tf_op jit(solution)/shard_map/ppermute | solution.py:36
  95.1 20.6 %collective-permute-start.33 = (bf16[256,1024]{1,0:T(8,128)(2,1)S(1)}, bf16[256,1024]{1,0:T(8,128)(2,1)S(1)}, u32[]{:S(2)}, u32[]{:S(2)}) collective-permute-start(bf16[256,1024]{1,0:T(8,128)(2,1)S(1)} %project_other.9), channel_id=1, source_target_pairs={{0,3},{1,2},{2,1},{3,0},{4,7},{5,6},{6,5},{7,4},{8,11},{9,10},{10,... | collective-permute-start | bytes 1572872 | tf_op jit(solution)/shard_map/ppermute | solution.py:36
  (16 other events, 79.1 us)

commit v3 on v2

--- a/solution.py
+++ b/solution.py
@@ -315,6 +315,31 @@
     )(*operands)
 
 
+def early_kernel(normed_ref, peer_ref, weight_ref, out_ref):
+    out_ref[...] = product(normed_ref, peer_ref, weight_ref)
+
+
+def finish_kernel(early_ref, received_ref, _, out_ref):
+    total = early_ref[...] + received_ref[...].astype(jnp.float32)
+    out_ref[...] = total.astype(jnp.bfloat16)
+
+
+def finish_last(early, received, place, target):
+    rows, features = early.shape
+    chunk = pl.BlockSpec((rows, features), lambda i: (0, 0))
+    return pl.pallas_call(
+        finish_kernel,
+        grid=(1,),
+        in_specs=[chunk, chunk, pl.BlockSpec(memory_space=pl.ANY)],
+        out_specs=pl.BlockSpec((rows, features), lambda i: (place // rows, 0)),
+        out_shape=jax.ShapeDtypeStruct(target.shape, target.dtype),
+        input_output_aliases={2: 0},
+        compiler_params=params(),
+        cost_estimate=COST,
+        name="finish_last",
+    )(early, received, target)
+
+
 def other_core(z, x, c, y):
     return z, x, 1 - c, y
 
@@ -531,9 +556,16 @@
     other(4, partial[3][0])
     own_weight = assemble(0, PAIR_BLOCKS, *after(tuple(own_lines), partial[4][0]))
     out = project_own(normed[:4], peers[:4], own_weight, received[:4], 0, tokens, None)
-    return project_own(
-        normed[4:], peers[4:], own_weight, received[4:], CHUNKS[4][0], tokens, out
-    )
+    early = small(
+        early_kernel,
+        jax.ShapeDtypeStruct(normed[4].shape, jnp.float32),
+        normed[4],
+        after(peers[4], out),
+        own_weight,
+        name="early_product",
+    )
+    back = after(received[4][0], early)
+    return finish_last(early, back, CHUNKS[4][0], out)
 
 
 def solution(mesh):

time: 118 us -> 121 us (1.025)
  waiting for transfers between devices: 37.5 us -> 40.2 us
    ppermute x35, waiting for transfers between devices: 37.5 us -> 40.2 us  [send(): return lax.ppermute(array, AXES, route(target))]
    pallas_call x2 -> x1, Pallas kernels: 6.61 us -> 4.57 us  [project_own(): pl.pallas_call(body, grid=(1,), in_specs=specs, out_specs=pl.BlockSpec((r...]
    pallas_call x7 -> x8, Pallas kernels: 1.17 us -> 2.41 us  [small(): pl.pallas_call(body, out_shape=shapes, compiler_params=params(), cost_est...]
where the time goes in v3:
time: 121 us
  starting transfers between devices  47.4 us (39%)
  waiting for transfers between devices  40.2 us (33%)
  Pallas kernels  29.4 us (24%)
  local copies, waits for them, and re-layouts  3.21 us (3%)
    ppermute x35, starting transfers between devices, send(): return lax.ppermute(array, AXES, route(target))  47.4 us
    ppermute x35, waiting for transfers between devices, send(): return lax.ppermute(array, AXES, route(target))  40.2 us
    pallas_call x4, Pallas kernels, local_part(): pl.pallas_call(local_kernel, grid=(features // width,), in_specs=[rows, s...  7.77 us
    pallas_call x5, Pallas kernels, project_other(): pl.pallas_call(other_kernel, out_shape=[out] * parts, compiler_params=par...  5.18 us
    pallas_call x1, Pallas kernels, project_own(): pl.pallas_call(body, grid=(1,), in_specs=specs, out_specs=pl.BlockSpec((r...  4.57 us
    pallas_call x2, Pallas kernels, assemble(): pl.pallas_call(functools.partial(assemble_kernel, home, blocks), in_specs...  3.47 us
    unnamed x10, local copies, waits for them, and re-layouts  3.19 us
    pallas_call x1, Pallas kernels, states(): pl.pallas_call(state_kernel, in_specs=[pl.BlockSpec(memory_space=pltpu.HB...  2.82 us
  transfers between devices with their start and end apart: 35, of which 14 were waited for; matrix products, arithmetic and copies ran while one was open for 0% of the time, Pallas kernels for 21%

profile of v3, /device:TPU:0, one launch (start us, length us, event | category | flops | bytes accessed | tf_op | source)
XLA Modules:
  0.0 120.7 jit_solution(17160577725976522542)
XLA Ops:
  3.2 2.8 %states.1 = (bf16[1024,1024]{1,0:T(8,128)(2,1)S(1)}, bf16[8,128,128]{2,1,0:T(8,128)(2,1)S(1)}, f32[8,128,128]{2,1,0:T(8,128)S(1)}) custom-call(bf16[1024,1024]{1,0:T(8,128)(2,1)S(1)} %copy-done.3, bf16[1024,1024]{1,0:T(8,128)(2,1)S(1)} %copy-done), custom_call_target="tpu_custom_call" | custom-call | flops 1 | bytes 1 | tf_op jit(solution)/shard_map/states/pallas_call | solution.py:88
  7.7 1.7 %collective-permute-start.1 = (bf16[4,128,128]{2,1,0:T(8,128)(2,1)S(1)}, bf16[4,128,128]{2,1,0:T(8,128)(2,1)S(1)}, u32[]{:S(2)}, u32[]{:S(2)}) collective-permute-start(bf16[4,128,128]{2,1,0:T(8,128)(2,1)S(1)} %get-tuple-element.67), channel_id=1, source_target_pairs={{0,8},{1,9},{2,10},{3,11},{4,12},{5,13},{6,14},{7,15},{8,0},{9,1},... | collective-permute-start | bytes 393224 | tf_op jit(solution)/shard_map/ppermute | solution.py:36
  9.4 4.1 %collective-permute-start.4 = (bf16[512,128]{1,0:T(8,128)(2,1)S(1)}, bf16[512,128]{1,0:T(8,128)(2,1)S(1)}, u32[]{:S(2)}, u32[]{:S(2)}) collective-permute-start(bf16[512,128]{1,0:T(8,128)(2,1)S(1)} %get-tuple-element.127), channel_id=1, source_target_pairs={{0,96},{1,64},{2,67},{3,99},{4,100},{5,68},{6,71},{7,103},{8,104},... | collective-permute-start | bytes 393224 | tf_op jit(solution)/shard_map/ppermute | solution.py:36
  15.8 2.2 %collective-permute-start.2 = (bf16[4,128,128]{2,1,0:T(8,128)(2,1)S(1)}, bf16[4,128,128]{2,1,0:T(8,128)(2,1)S(1)}, u32[]{:S(2)}, u32[]{:S(2)}) collective-permute-start(bf16[4,128,128]{2,1,0:T(8,128)(2,1)S(1)} %get-tuple-element.76), channel_id=1, source_target_pairs={{0,24},{1,25},{2,26},{3,27},{4,28},{5,29},{6,30},{7,31},{8,16},{9,... | collective-permute-start | bytes 393224 | tf_op jit(solution)/shard_map/ppermute | solution.py:36
  18.1 4.0 %collective-permute-done.2.refs_2_ = bf16[4,128,128]{2,1,0:T(8,128)(2,1)S(1)} collective-permute-done((bf16[4,128,128]{2,1,0:T(8,128)(2,1)S(1)}, bf16[4,128,128]{2,1,0:T(8,128)(2,1)S(1)}, u32[]{:S(2)}, u32[]{:S(2)}) %collective-permute-start.2) | collective-permute-done | bytes 131104 | tf_op jit(solution)/shard_map/ppermute | solution.py:36
  22.1 4.1 %collective-permute-start.5 = (bf16[4,128,128]{2,1,0:T(8,128)(2,1)S(1)}, bf16[4,128,128]{2,1,0:T(8,128)(2,1)S(1)}, u32[]{:S(2)}, u32[]{:S(2)}) collective-permute-start(bf16[4,128,128]{2,1,0:T(8,128)(2,1)S(1)} %get-tuple-element.84), channel_id=1, source_target_pairs={{0,32},{1,33},{2,34},{3,35},{4,36},{5,37},{6,38},{7,39},{8,40},{9,... | collective-permute-start | bytes 393224 | tf_op jit(solution)/shard_map/ppermute | solution.py:36
  29.2 1.8 %collective-permute-start.7 = (bf16[512,128]{1,0:T(8,128)(2,1)S(1)}, bf16[512,128]{1,0:T(8,128)(2,1)S(1)}, u32[]{:S(2)}, u32[]{:S(2)}) collective-permute-start(bf16[512,128]{1,0:T(8,128)(2,1)S(1)} %get-tuple-element.87), channel_id=1, source_target_pairs={{0,24},{1,25},{2,26},{3,27},{4,100},{5,101},{6,102},{7,103},{8,0},... | collective-permute-start | bytes 393224 | tf_op jit(solution)/shard_map/ppermute | solution.py:36
  36.0 2.8 %collective-permute-start.12 = (bf16[4,512,128]{2,1,0:T(8,128)(2,1)S(1)}, bf16[4,512,128]{2,1,0:T(8,128)(2,1)S(1)}, u32[]{:S(2)}, u32[]{:S(2)}) collective-permute-start(bf16[4,512,128]{2,1,0:T(8,128)(2,1)S(1)} %pad_maximum_fusion.1.refs_0_), channel_id=1, source_target_pairs={{0,96},{1,97},{2,98},{3,99},{4,28},{5,29},{6,30},{7,31},{8,104},{9... | collective-permute-start | bytes 1572872 | tf_op jit(solution)/shard_map/ppermute | solution.py:36
  43.4 2.3 %local_part.5 = (f32[256,1024]{1,0:T(8,128)S(1)}, bf16[256,1024]{1,0:T(8,128)(2,1)S(1)}) custom-call(bf16[1024,1024]{1,0:T(8,128)(2,1)S(1)} %copy-done.2, bf16[1024,1024]{1,0:T(8,128)(2,1)S(1)} %get-tuple-element.69.feat_ref, bf16[1024,1024]{1,0:T(8,128)(2,1)S(1)} %copy-done.1), custom_call_target="tpu_custom_call" | custom-call | flops 1 | bytes 1 | tf_op jit(solution)/shard_map/local_part/pallas_call | solution.py:140
  48.3 2.3 %collective-permute-done.13.refs_2_ = bf16[4,512,128]{2,1,0:T(8,128)(2,1)S(1)} collective-permute-done((bf16[4,512,128]{2,1,0:T(8,128)(2,1)S(1)}, bf16[4,512,128]{2,1,0:T(8,128)(2,1)S(1)}, u32[]{:S(2)}, u32[]{:S(2)}) %collective-permute-start.13) | collective-permute-done | bytes 524320 | tf_op jit(solution)/shard_map/ppermute | solution.py:36
  51.6 3.3 %collective-permute-done.21.peer_ref.refs_5_ = bf16[128,1024]{1,0:T(8,128)(2,1)S(1)} collective-permute-done((bf16[128,1024]{1,0:T(8,128)(2,1)S(1)}, bf16[128,1024]{1,0:T(8,128)(2,1)S(1)}, u32[]{:S(2)}, u32[]{:S(2)}) %collective-permute-start.21) | collective-permute-done | bytes 262176 | tf_op jit(solution)/shard_map/ppermute | solution.py:36
  56.2 1.9 %assemble.2.weight_ref = bf16[2,1024,1024]{2,1,0:T(8,128)(2,1)S(1)} custom-call(bf16[4,512,128]{2,1,0:T(8,128)(2,1)S(1)} %pad_maximum_fusion.1.refs_0_, bf16[4,512,128]{2,1,0:T(8,128)(2,1)S(1)} %collective-permute-done.12.refs_1_, bf16[4,512,128]{2,1,0:T(8,128)(2,1)S(1)} %collective-permute-done.13.refs_2_, ...), custom_call_target="tpu_custom_call" | custom-call | flops 1 | bytes 1 | tf_op jit(solution)/shard_map/assemble/pallas_call | solution.py:236
  58.8 2.3 %collective-permute-start.23 = (bf16[128,1024]{1,0:T(8,128)(2,1)S(1)}, bf16[128,1024]{1,0:T(8,128)(2,1)S(1)}, u32[]{:S(2)}, u32[]{:S(2)}) collective-permute-start(bf16[128,1024]{1,0:T(8,128)(2,1)S(1)} %project_other.5), channel_id=1, source_target_pairs={{0,3},{1,2},{2,1},{3,0},{4,7},{5,6},{6,5},{7,4},{8,11},{9,10},{10,... | collective-permute-start | bytes 786440 | tf_op jit(solution)/shard_map/ppermute | solution.py:36
  61.0 2.3 %local_part.7 = (f32[256,1024]{1,0:T(8,128)S(1)}, bf16[256,1024]{1,0:T(8,128)(2,1)S(1)}) custom-call(bf16[1024,1024]{1,0:T(8,128)(2,1)S(1)} %copy-done.2, bf16[1024,1024]{1,0:T(8,128)(2,1)S(1)} %get-tuple-element.69.feat_ref, bf16[1024,1024]{1,0:T(8,128)(2,1)S(1)} %copy-done.1), custom_call_target="tpu_custom_call" | custom-call | flops 1 | bytes 1 | tf_op jit(solution)/shard_map/local_part/pallas_call | solution.py:140
  69.5 1.9 %collective-permute-start.27 = (bf16[2,512,128]{2,1,0:T(8,128)(2,1)S(1)}, bf16[2,512,128]{2,1,0:T(8,128)(2,1)S(1)}, u32[]{:S(2)}, u32[]{:S(2)}) collective-permute-start(bf16[2,512,128]{2,1,0:T(8,128)(2,1)S(1)} %pad_maximum_fusion.2), channel_id=1, source_target_pairs={{0,24},{1,25},{2,26},{3,27},{4,100},{5,101},{6,102},{7,103},{8,0},... | collective-permute-start | bytes 786440 | tf_op jit(solution)/shard_map/ppermute | solution.py:36
  72.7 2.7 %collective-permute-done.24.refs_10_ = bf16[128,1024]{1,0:T(8,128)(2,1)S(1)} collective-permute-done((bf16[128,1024]{1,0:T(8,128)(2,1)S(1)}, bf16[128,1024]{1,0:T(8,128)(2,1)S(1)}, u32[]{:S(2)}, u32[]{:S(2)}) %collective-permute-start.24) | collective-permute-done | bytes 262176 | tf_op jit(solution)/shard_map/ppermute | solution.py:36
  75.3 1.9 %collective-permute-done.28 = bf16[2,512,128]{2,1,0:T(8,128)(2,1)S(1)} collective-permute-done((bf16[2,512,128]{2,1,0:T(8,128)(2,1)S(1)}, bf16[2,512,128]{2,1,0:T(8,128)(2,1)S(1)}, u32[]{:S(2)}, u32[]{:S(2)}) %collective-permute-start.28) | collective-permute-done | bytes 262176 | tf_op jit(solution)/shard_map/ppermute | solution.py:36
  79.8 2.3 %collective-permute-start.30 = (bf16[4,2,512,128]{3,2,1,0:T(8,128)(2,1)S(1)}, bf16[4,2,512,128]{3,2,1,0:T(8,128)(2,1)S(1)}, u32[]{:S(2)}, u32[]{:S(2)}) collective-permute-start(bf16[4,2,512,128]{3,2,1,0:T(8,128)(2,1)S(1)} %pad_maximum_fusion.refs_0_), channel_id=1, source_target_pairs={{0,96},{1,97},{2,98},{3,99},{4,28},{5,29},{6,30},{7,31},{8,104},{9... | collective-permute-start | bytes 3145736 | tf_op jit(solution)/shard_map/ppermute | solution.py:36
  82.0 2.8 %collective-permute-start.25 = (bf16[256,1024]{1,0:T(8,128)(2,1)S(1)}, bf16[256,1024]{1,0:T(8,128)(2,1)S(1)}, u32[]{:S(2)}, u32[]{:S(2)}) collective-permute-start(bf16[256,1024]{1,0:T(8,128)(2,1)S(1)} %project_other.6), channel_id=1, source_target_pairs={{0,3},{1,2},{2,1},{3,0},{4,7},{5,6},{6,5},{7,4},{8,11},{9,10},{10,... | collective-permute-start | bytes 1572872 | tf_op jit(solution)/shard_map/ppermute | solution.py:36
  84.8 10.2 %collective-permute-done.25.refs_11_ = bf16[256,1024]{1,0:T(8,128)(2,1)S(1)} collective-permute-done((bf16[256,1024]{1,0:T(8,128)(2,1)S(1)}, bf16[256,1024]{1,0:T(8,128)(2,1)S(1)}, u32[]{:S(2)}, u32[]{:S(2)}) %collective-permute-start.25) | collective-permute-done | bytes 524320 | tf_op jit(solution)/shard_map/ppermute | solution.py:36
  96.3 2.7 %collective-permute-start.33 = (bf16[256,1024]{1,0:T(8,128)(2,1)S(1)}, bf16[256,1024]{1,0:T(8,128)(2,1)S(1)}, u32[]{:S(2)}, u32[]{:S(2)}) collective-permute-start(bf16[256,1024]{1,0:T(8,128)(2,1)S(1)} %project_other.8), channel_id=1, source_target_pairs={{0,3},{1,2},{2,1},{3,0},{4,7},{5,6},{6,5},{7,4},{8,11},{9,10},{10,... | collective-permute-start | bytes 1572872 | tf_op jit(solution)/shard_map/ppermute | solution.py:36
  101.2 3.7 %collective-permute-done.31.refs_2_ = bf16[4,2,512,128]{3,2,1,0:T(8,128)(2,1)S(1)} collective-permute-done((bf16[4,2,512,128]{3,2,1,0:T(8,128)(2,1)S(1)}, bf16[4,2,512,128]{3,2,1,0:T(8,128)(2,1)S(1)}, u32[]{:S(2)}, u32[]{:S(2)}) %collective-permute-start.31) | collective-permute-done | bytes 1048608 | tf_op jit(solution)/shard_map/ppermute | solution.py:36
  106.6 5.9 %collective-permute-done.33.refs_12_ = bf16[256,1024]{1,0:T(8,128)(2,1)S(1)} collective-permute-done((bf16[256,1024]{1,0:T(8,128)(2,1)S(1)}, bf16[256,1024]{1,0:T(8,128)(2,1)S(1)}, u32[]{:S(2)}, u32[]{:S(2)}) %collective-permute-start.33) | collective-permute-done | bytes 524320 | tf_op jit(solution)/shard_map/ppermute | solution.py:36
  112.5 4.6 %project_own.1._ = bf16[1024,1024]{1,0:T(8,128)(2,1)} custom-call(bf16[128,1024]{1,0:T(8,128)(2,1)S(1)} %norm_part.5.normed_ref.refs_0_, bf16[128,1024]{1,0:T(8,128)(2,1)S(1)} %norm_part.6.normed_ref.refs_1_, bf16[256,1024]{1,0:T(8,128)(2,1)S(1)} %norm_part.7.normed_ref.refs_2_, bf16[256,1024]{1,0:T(8,128)(2,1)S(1)} %norm_part.8.normed_ref.refs_3_, ...), custom_call_target="tpu_custom_call" | custom-call | flops 1 | bytes 1 | tf_op jit(solution)/shard_map/project_own/pallas_call | solution.py:305
  (87 shorter events, 43.9 us)
Async XLA Ops:
  7.7 8.1 %collective-permute-start.1 = (bf16[4,128,128]{2,1,0:T(8,128)(2,1)S(1)}, bf16[4,128,128]{2,1,0:T(8,128)(2,1)S(1)}, u32[]{:S(2)}, u32[]{:S(2)}) collective-permute-start(bf16[4,128,128]{2,1,0:T(8,128)(2,1)S(1)} %get-tuple-element.67), channel_id=1, source_target_pairs={{0,8},{1,9},{2,10},{3,11},{4,12},{5,13},{6,14},{7,15},{8,0},{9,1},... | collective-permute-start | bytes 393224 | tf_op jit(solution)/shard_map/ppermute | solution.py:36
  9.4 8.6 %collective-permute-start.4 = (bf16[512,128]{1,0:T(8,128)(2,1)S(1)}, bf16[512,128]{1,0:T(8,128)(2,1)S(1)}, u32[]{:S(2)}, u32[]{:S(2)}) collective-permute-start(bf16[512,128]{1,0:T(8,128)(2,1)S(1)} %get-tuple-element.127), channel_id=1, source_target_pairs={{0,96},{1,64},{2,67},{3,99},{4,100},{5,68},{6,71},{7,103},{8,104},... | collective-permute-start | bytes 393224 | tf_op jit(solution)/shard_map/ppermute | solution.py:36
  22.1 8.8 %collective-permute-start.5 = (bf16[4,128,128]{2,1,0:T(8,128)(2,1)S(1)}, bf16[4,128,128]{2,1,0:T(8,128)(2,1)S(1)}, u32[]{:S(2)}, u32[]{:S(2)}) collective-permute-start(bf16[4,128,128]{2,1,0:T(8,128)(2,1)S(1)} %get-tuple-element.84), channel_id=1, source_target_pairs={{0,32},{1,33},{2,34},{3,35},{4,36},{5,37},{6,38},{7,39},{8,40},{9,... | collective-permute-start | bytes 393224 | tf_op jit(solution)/shard_map/ppermute | solution.py:36
  26.2 6.5 %collective-permute-start.9 = (bf16[512,128]{1,0:T(8,128)(2,1)S(1)}, bf16[512,128]{1,0:T(8,128)(2,1)S(1)}, u32[]{:S(2)}, u32[]{:S(2)}) collective-permute-start(bf16[512,128]{1,0:T(8,128)(2,1)S(1)} %get-tuple-element.87), channel_id=1, source_target_pairs={{0,16},{1,17},{2,18},{3,19},{4,68},{5,69},{6,70},{7,71},{8,24},{9,... | collective-permute-start | bytes 393224 | tf_op jit(solution)/shard_map/ppermute | solution.py:36
  31.7 7.1 %collective-permute-start.6 = (bf16[4,128,128]{2,1,0:T(8,128)(2,1)S(1)}, bf16[4,128,128]{2,1,0:T(8,128)(2,1)S(1)}, u32[]{:S(2)}, u32[]{:S(2)}) collective-permute-start(bf16[4,128,128]{2,1,0:T(8,128)(2,1)S(1)} %get-tuple-element.86), channel_id=1, source_target_pairs={{0,96},{1,97},{2,98},{3,99},{4,100},{5,101},{6,102},{7,103},{8,104... | collective-permute-start | bytes 393224 | tf_op jit(solution)/shard_map/ppermute | solution.py:36
  34.2 14.1 %collective-permute-start.14 = (bf16[4,512,128]{2,1,0:T(8,128)(2,1)S(1)}, bf16[4,512,128]{2,1,0:T(8,128)(2,1)S(1)}, u32[]{:S(2)}, u32[]{:S(2)}) collective-permute-start(bf16[4,512,128]{2,1,0:T(8,128)(2,1)S(1)} %pad_maximum_fusion.1.refs_0_), channel_id=1, source_target_pairs={{0,64},{1,65},{2,66},{3,67},{4,20},{5,21},{6,22},{7,23},{8,72},{9,... | collective-permute-start | bytes 1572872 | tf_op jit(solution)/shard_map/ppermute | solution.py:36
  35.6 15.0 %collective-permute-start.13 = (bf16[4,512,128]{2,1,0:T(8,128)(2,1)S(1)}, bf16[4,512,128]{2,1,0:T(8,128)(2,1)S(1)}, u32[]{:S(2)}, u32[]{:S(2)}) collective-permute-start(bf16[4,512,128]{2,1,0:T(8,128)(2,1)S(1)} %pad_maximum_fusion.1.refs_0_), channel_id=1, source_target_pairs={{0,32},{1,33},{2,34},{3,35},{4,12},{5,13},{6,14},{7,15},{8,40},{9,... | collective-permute-start | bytes 1572872 | tf_op jit(solution)/shard_map/ppermute | solution.py:36
  36.0 14.6 %collective-permute-start.12 = (bf16[4,512,128]{2,1,0:T(8,128)(2,1)S(1)}, bf16[4,512,128]{2,1,0:T(8,128)(2,1)S(1)}, u32[]{:S(2)}, u32[]{:S(2)}) collective-permute-start(bf16[4,512,128]{2,1,0:T(8,128)(2,1)S(1)} %pad_maximum_fusion.1.refs_0_), channel_id=1, source_target_pairs={{0,96},{1,97},{2,98},{3,99},{4,28},{5,29},{6,30},{7,31},{8,104},{9... | collective-permute-start | bytes 1572872 | tf_op jit(solution)/shard_map/ppermute | solution.py:36
  40.8 9.8 %collective-permute-start.11 = (bf16[128,1024]{1,0:T(8,128)(2,1)S(1)}, bf16[128,1024]{1,0:T(8,128)(2,1)S(1)}, u32[]{:S(2)}, u32[]{:S(2)}) collective-permute-start(bf16[128,1024]{1,0:T(8,128)(2,1)S(1)} %norm_part.5.normed_ref.refs_0_), channel_id=1, source_target_pairs={{0,1},{1,0},{2,3},{3,2},{4,5},{5,4},{6,7},{7,6},{8,9},{9,8},{10,11... | collective-permute-start | bytes 786440 | tf_op jit(solution)/shard_map/ppermute | solution.py:36
  42.5 12.3 %collective-permute-start.21 = (bf16[128,1024]{1,0:T(8,128)(2,1)S(1)}, bf16[128,1024]{1,0:T(8,128)(2,1)S(1)}, u32[]{:S(2)}, u32[]{:S(2)}) collective-permute-start(bf16[128,1024]{1,0:T(8,128)(2,1)S(1)} %norm_part.6.normed_ref.refs_1_), channel_id=1, source_target_pairs={{0,1},{1,0},{2,3},{3,2},{4,5},{5,4},{6,7},{7,6},{8,9},{9,8},{10,11... | collective-permute-start | bytes 786440 | tf_op jit(solution)/shard_map/ppermute | solution.py:36
  54.9 13.3 %collective-permute-start.22 = (bf16[256,1024]{1,0:T(8,128)(2,1)S(1)}, bf16[256,1024]{1,0:T(8,128)(2,1)S(1)}, u32[]{:S(2)}, u32[]{:S(2)}) collective-permute-start(bf16[256,1024]{1,0:T(8,128)(2,1)S(1)} %norm_part.7.normed_ref.refs_2_), channel_id=1, source_target_pairs={{0,1},{1,0},{2,3},{3,2},{4,5},{5,4},{6,7},{7,6},{8,9},{9,8},{10,11... | collective-permute-start | bytes 1572872 | tf_op jit(solution)/shard_map/ppermute | solution.py:36
  58.8 10.7 %collective-permute-start.23 = (bf16[128,1024]{1,0:T(8,128)(2,1)S(1)}, bf16[128,1024]{1,0:T(8,128)(2,1)S(1)}, u32[]{:S(2)}, u32[]{:S(2)}) collective-permute-start(bf16[128,1024]{1,0:T(8,128)(2,1)S(1)} %project_other.5), channel_id=1, source_target_pairs={{0,3},{1,2},{2,1},{3,0},{4,7},{5,6},{6,5},{7,4},{8,11},{9,10},{10,... | collective-permute-start | bytes 786440 | tf_op jit(solution)/shard_map/ppermute | solution.py:36
  64.7 20.1 %collective-permute-start.20 = (bf16[256,1024]{1,0:T(8,128)(2,1)S(1)}, bf16[256,1024]{1,0:T(8,128)(2,1)S(1)}, u32[]{:S(2)}, u32[]{:S(2)}) collective-permute-start(bf16[256,1024]{1,0:T(8,128)(2,1)S(1)} %norm_part.8.normed_ref.refs_3_), channel_id=1, source_target_pairs={{0,1},{1,0},{2,3},{3,2},{4,5},{5,4},{6,7},{7,6},{8,9},{9,8},{10,11... | collective-permute-start | bytes 1572872 | tf_op jit(solution)/shard_map/ppermute | solution.py:36
  65.8 9.6 %collective-permute-start.24 = (bf16[128,1024]{1,0:T(8,128)(2,1)S(1)}, bf16[128,1024]{1,0:T(8,128)(2,1)S(1)}, u32[]{:S(2)}, u32[]{:S(2)}) collective-permute-start(bf16[128,1024]{1,0:T(8,128)(2,1)S(1)} %project_other.7), channel_id=1, source_target_pairs={{0,3},{1,2},{2,1},{3,0},{4,7},{5,6},{6,5},{7,4},{8,11},{9,10},{10,... | collective-permute-start | bytes 786440 | tf_op jit(solution)/shard_map/ppermute | solution.py:36
  66.4 8.9 %collective-permute-start.29 = (bf16[2,512,128]{2,1,0:T(8,128)(2,1)S(1)}, bf16[2,512,128]{2,1,0:T(8,128)(2,1)S(1)}, u32[]{:S(2)}, u32[]{:S(2)}) collective-permute-start(bf16[2,512,128]{2,1,0:T(8,128)(2,1)S(1)} %pad_maximum_fusion.2), channel_id=1, source_target_pairs={{0,16},{1,17},{2,18},{3,19},{4,68},{5,69},{6,70},{7,71},{8,24},{9,... | collective-permute-start | bytes 786440 | tf_op jit(solution)/shard_map/ppermute | solution.py:36
  68.2 9.0 %collective-permute-start.28 = (bf16[2,512,128]{2,1,0:T(8,128)(2,1)S(1)}, bf16[2,512,128]{2,1,0:T(8,128)(2,1)S(1)}, u32[]{:S(2)}, u32[]{:S(2)}) collective-permute-start(bf16[2,512,128]{2,1,0:T(8,128)(2,1)S(1)} %pad_maximum_fusion.2), channel_id=1, source_target_pairs={{0,8},{1,9},{2,10},{3,11},{4,36},{5,37},{6,38},{7,39},{8,16},{9,17... | collective-permute-start | bytes 786440 | tf_op jit(solution)/shard_map/ppermute | solution.py:36
  69.5 7.7 %collective-permute-start.27 = (bf16[2,512,128]{2,1,0:T(8,128)(2,1)S(1)}, bf16[2,512,128]{2,1,0:T(8,128)(2,1)S(1)}, u32[]{:S(2)}, u32[]{:S(2)}) collective-permute-start(bf16[2,512,128]{2,1,0:T(8,128)(2,1)S(1)} %pad_maximum_fusion.2), channel_id=1, source_target_pairs={{0,24},{1,25},{2,26},{3,27},{4,100},{5,101},{6,102},{7,103},{8,0},... | collective-permute-start | bytes 786440 | tf_op jit(solution)/shard_map/ppermute | solution.py:36
  77.3 23.9 %collective-permute-start.32 = (bf16[4,2,512,128]{3,2,1,0:T(8,128)(2,1)S(1)}, bf16[4,2,512,128]{3,2,1,0:T(8,128)(2,1)S(1)}, u32[]{:S(2)}, u32[]{:S(2)}) collective-permute-start(bf16[4,2,512,128]{3,2,1,0:T(8,128)(2,1)S(1)} %pad_maximum_fusion.refs_0_), channel_id=1, source_target_pairs={{0,64},{1,65},{2,66},{3,67},{4,20},{5,21},{6,22},{7,23},{8,72},{9,... | collective-permute-start | bytes 3145736 | tf_op jit(solution)/shard_map/ppermute | solution.py:36
  78.8 26.1 %collective-permute-start.31 = (bf16[4,2,512,128]{3,2,1,0:T(8,128)(2,1)S(1)}, bf16[4,2,512,128]{3,2,1,0:T(8,128)(2,1)S(1)}, u32[]{:S(2)}, u32[]{:S(2)}) collective-permute-start(bf16[4,2,512,128]{3,2,1,0:T(8,128)(2,1)S(1)} %pad_maximum_fusion.refs_0_), channel_id=1, source_target_pairs={{0,32},{1,33},{2,34},{3,35},{4,12},{5,13},{6,14},{7,15},{8,40},{9,... | collective-permute-start | bytes 3145736 | tf_op jit(solution)/shard_map/ppermute | solution.py:36
  79.8 25.2 %collective-permute-start.30 = (bf16[4,2,512,128]{3,2,1,0:T(8,128)(2,1)S(1)}, bf16[4,2,512,128]{3,2,1,0:T(8,128)(2,1)S(1)}, u32[]{:S(2)}, u32[]{:S(2)}) collective-permute-start(bf16[4,2,512,128]{3,2,1,0:T(8,128)(2,1)S(1)} %pad_maximum_fusion.refs_0_), channel_id=1, source_target_pairs={{0,96},{1,97},{2,98},{3,99},{4,28},{5,29},{6,30},{7,31},{8,104},{9... | collective-permute-start | bytes 3145736 | tf_op jit(solution)/shard_map/ppermute | solution.py:36
  82.0 13.0 %collective-permute-start.25 = (bf16[256,1024]{1,0:T(8,128)(2,1)S(1)}, bf16[256,1024]{1,0:T(8,128)(2,1)S(1)}, u32[]{:S(2)}, u32[]{:S(2)}) collective-permute-start(bf16[256,1024]{1,0:T(8,128)(2,1)S(1)} %project_other.6), channel_id=1, source_target_pairs={{0,3},{1,2},{2,1},{3,0},{4,7},{5,6},{6,5},{7,4},{8,11},{9,10},{10,... | collective-permute-start | bytes 1572872 | tf_op jit(solution)/shard_map/ppermute | solution.py:36
  84.8 14.2 %collective-permute-start.19 = (bf16[256,1024]{1,0:T(8,128)(2,1)S(1)}, bf16[256,1024]{1,0:T(8,128)(2,1)S(1)}, u32[]{:S(2)}, u32[]{:S(2)}) collective-permute-start(bf16[256,1024]{1,0:T(8,128)(2,1)S(1)} %norm_part.9.normed_ref), channel_id=1, source_target_pairs={{0,1},{1,0},{2,3},{3,2},{4,5},{5,4},{6,7},{7,6},{8,9},{9,8},{10,11... | collective-permute-start | bytes 1572872 | tf_op jit(solution)/shard_map/ppermute | solution.py:36
  96.3 16.1 %collective-permute-start.33 = (bf16[256,1024]{1,0:T(8,128)(2,1)S(1)}, bf16[256,1024]{1,0:T(8,128)(2,1)S(1)}, u32[]{:S(2)}, u32[]{:S(2)}) collective-permute-start(bf16[256,1024]{1,0:T(8,128)(2,1)S(1)} %project_other.8), channel_id=1, source_target_pairs={{0,3},{1,2},{2,1},{3,0},{4,7},{5,6},{6,5},{7,4},{8,11},{9,10},{10,... | collective-permute-start | bytes 1572872 | tf_op jit(solution)/shard_map/ppermute | solution.py:36
  100.3 19.5 %collective-permute-start.34 = (bf16[256,1024]{1,0:T(8,128)(2,1)S(1)}, bf16[256,1024]{1,0:T(8,128)(2,1)S(1)}, u32[]{:S(2)}, u32[]{:S(2)}) collective-permute-start(bf16[256,1024]{1,0:T(8,128)(2,1)S(1)} %project_other.9), channel_id=1, source_target_pairs={{0,3},{1,2},{2,1},{3,0},{4,7},{5,6},{6,5},{7,4},{8,11},{9,10},{10,... | collective-permute-start | bytes 1572872 | tf_op jit(solution)/shard_map/ppermute | solution.py:36
  (16 other events, 79.1 us)

commit v4 on v2

--- a/solution.py
+++ b/solution.py
@@ -523,7 +523,7 @@
     other(0)
     norm(4, partial[0][0])
     other(1, normed[4])
-    own_pair = jnp.stack([own_item, send(after(own_item, partial[1][0]), other_core)])
+    own_pair = jnp.stack([own_item, send(after(own_item, partial[1][0], received[0][0]), other_core)])
     own_line = first_moves(own_pair)
     other(2, received[0][0], normed[4])
     own_lines = second_moves(jnp.stack(after(tuple(own_line), partial[2][0], received[1][0])))

time: 118 us -> 125 us (1.059)
  waiting for transfers between devices: 37.5 us -> 41.7 us
  starting transfers between devices: 47.2 us -> 50 us
    ppermute x35, waiting for transfers between devices: 37.5 us -> 41.7 us  [send(): return lax.ppermute(array, AXES, route(target))]
    ppermute x35, starting transfers between devices: 47.2 us -> 50 us  [send(): return lax.ppermute(array, AXES, route(target))]
  transfers between devices with their start and end apart: 35 -> 35, of which waited for: 14 -> 15; matrix products, arithmetic and copies ran while one was open for 0% -> 0% of each run, Pallas kernels for 21% -> 20%
where the time goes in v4:
time: 125 us
  starting transfers between devices  50 us (40%)
  waiting for transfers between devices  41.7 us (33%)
  Pallas kernels  29.3 us (23%)
  local copies, waits for them, and re-layouts  3.21 us (3%)
    ppermute x35, starting transfers between devices, send(): return lax.ppermute(array, AXES, route(target))  50 us
    ppermute x35, waiting for transfers between devices, send(): return lax.ppermute(array, AXES, route(target))  41.7 us
    pallas_call x4, Pallas kernels, local_part(): pl.pallas_call(local_kernel, grid=(features // width,), in_specs=[rows, s...  7.79 us
    pallas_call x2, Pallas kernels, project_own(): pl.pallas_call(body, grid=(1,), in_specs=specs, out_specs=pl.BlockSpec((r...  6.62 us
    pallas_call x5, Pallas kernels, project_other(): pl.pallas_call(other_kernel, out_shape=[out] * parts, compiler_params=par...  5.19 us
    pallas_call x2, Pallas kernels, assemble(): pl.pallas_call(functools.partial(assemble_kernel, home, blocks), in_specs...  3.47 us
    unnamed x10, local copies, waits for them, and re-layouts  3.19 us
    pallas_call x1, Pallas kernels, states(): pl.pallas_call(state_kernel, in_specs=[pl.BlockSpec(memory_space=pltpu.HB...  2.82 us
  transfers between devices with their start and end apart: 35, of which 15 were waited for; matrix products, arithmetic and copies ran while one was open for 0% of the time, Pallas kernels for 20%

profile of v4, /device:TPU:0, one launch (start us, length us, event | category | flops | bytes accessed | tf_op | source)
XLA Modules:
  0.0 124.7 jit_solution(10216583112125737948)
XLA Ops:
  3.2 2.8 %states.1 = (bf16[1024,1024]{1,0:T(8,128)(2,1)S(1)}, bf16[8,128,128]{2,1,0:T(8,128)(2,1)S(1)}, f32[8,128,128]{2,1,0:T(8,128)S(1)}) custom-call(bf16[1024,1024]{1,0:T(8,128)(2,1)S(1)} %copy-done.3, bf16[1024,1024]{1,0:T(8,128)(2,1)S(1)} %copy-done), custom_call_target="tpu_custom_call" | custom-call | flops 1 | bytes 1 | tf_op jit(solution)/shard_map/states/pallas_call | solution.py:88
  9.4 4.1 %collective-permute-start.4 = (bf16[512,128]{1,0:T(8,128)(2,1)S(1)}, bf16[512,128]{1,0:T(8,128)(2,1)S(1)}, u32[]{:S(2)}, u32[]{:S(2)}) collective-permute-start(bf16[512,128]{1,0:T(8,128)(2,1)S(1)} %get-tuple-element.123), channel_id=1, source_target_pairs={{0,96},{1,64},{2,67},{3,99},{4,100},{5,68},{6,71},{7,103},{8,104},... | collective-permute-start | bytes 393224 | tf_op jit(solution)/shard_map/ppermute | solution.py:36
  15.8 2.2 %collective-permute-start.2 = (bf16[4,128,128]{2,1,0:T(8,128)(2,1)S(1)}, bf16[4,128,128]{2,1,0:T(8,128)(2,1)S(1)}, u32[]{:S(2)}, u32[]{:S(2)}) collective-permute-start(bf16[4,128,128]{2,1,0:T(8,128)(2,1)S(1)} %get-tuple-element.74), channel_id=1, source_target_pairs={{0,24},{1,25},{2,26},{3,27},{4,28},{5,29},{6,30},{7,31},{8,16},{9,... | collective-permute-start | bytes 393224 | tf_op jit(solution)/shard_map/ppermute | solution.py:36
  18.1 4.0 %collective-permute-done.2.refs_2_ = bf16[4,128,128]{2,1,0:T(8,128)(2,1)S(1)} collective-permute-done((bf16[4,128,128]{2,1,0:T(8,128)(2,1)S(1)}, bf16[4,128,128]{2,1,0:T(8,128)(2,1)S(1)}, u32[]{:S(2)}, u32[]{:S(2)}) %collective-permute-start.2) | collective-permute-done | bytes 131104 | tf_op jit(solution)/shard_map/ppermute | solution.py:36
  22.1 4.1 %collective-permute-start.5 = (bf16[4,128,128]{2,1,0:T(8,128)(2,1)S(1)}, bf16[4,128,128]{2,1,0:T(8,128)(2,1)S(1)}, u32[]{:S(2)}, u32[]{:S(2)}) collective-permute-start(bf16[4,128,128]{2,1,0:T(8,128)(2,1)S(1)} %get-tuple-element.82), channel_id=1, source_target_pairs={{0,32},{1,33},{2,34},{3,35},{4,36},{5,37},{6,38},{7,39},{8,40},{9,... | collective-permute-start | bytes 393224 | tf_op jit(solution)/shard_map/ppermute | solution.py:36
  36.0 2.8 %collective-permute-start.12 = (bf16[4,512,128]{2,1,0:T(8,128)(2,1)S(1)}, bf16[4,512,128]{2,1,0:T(8,128)(2,1)S(1)}, u32[]{:S(2)}, u32[]{:S(2)}) collective-permute-start(bf16[4,512,128]{2,1,0:T(8,128)(2,1)S(1)} %pad_maximum_fusion.1.refs_0_), channel_id=1, source_target_pairs={{0,96},{1,97},{2,98},{3,99},{4,28},{5,29},{6,30},{7,31},{8,104},{9... | collective-permute-start | bytes 1572872 | tf_op jit(solution)/shard_map/ppermute | solution.py:36
  42.5 2.3 %local_part.5 = (f32[256,1024]{1,0:T(8,128)S(1)}, bf16[256,1024]{1,0:T(8,128)(2,1)S(1)}) custom-call(bf16[1024,1024]{1,0:T(8,128)(2,1)S(1)} %copy-done.2, bf16[1024,1024]{1,0:T(8,128)(2,1)S(1)} %get-tuple-element.67.feat_ref, bf16[1024,1024]{1,0:T(8,128)(2,1)S(1)} %copy-done.1), custom_call_target="tpu_custom_call" | custom-call | flops 1 | bytes 1 | tf_op jit(solution)/shard_map/local_part/pallas_call | solution.py:140
  47.5 3.1 %collective-permute-done.13.refs_2_ = bf16[4,512,128]{2,1,0:T(8,128)(2,1)S(1)} collective-permute-done((bf16[4,512,128]{2,1,0:T(8,128)(2,1)S(1)}, bf16[4,512,128]{2,1,0:T(8,128)(2,1)S(1)}, u32[]{:S(2)}, u32[]{:S(2)}) %collective-permute-start.13) | collective-permute-done | bytes 524320 | tf_op jit(solution)/shard_map/ppermute | solution.py:36
  52.3 7.6 %collective-permute-done.21.peer_ref.refs_5_ = bf16[128,1024]{1,0:T(8,128)(2,1)S(1)} collective-permute-done((bf16[128,1024]{1,0:T(8,128)(2,1)S(1)}, bf16[128,1024]{1,0:T(8,128)(2,1)S(1)}, u32[]{:S(2)}, u32[]{:S(2)}) %collective-permute-start.21) | collective-permute-done | bytes 262176 | tf_op jit(solution)/shard_map/ppermute | solution.py:36
  60.7 1.9 %assemble.2.weight_ref = bf16[2,1024,1024]{2,1,0:T(8,128)(2,1)S(1)} custom-call(bf16[4,512,128]{2,1,0:T(8,128)(2,1)S(1)} %pad_maximum_fusion.1.refs_0_, bf16[4,512,128]{2,1,0:T(8,128)(2,1)S(1)} %collective-permute-done.12.refs_1_, bf16[4,512,128]{2,1,0:T(8,128)(2,1)S(1)} %collective-permute-done.13.refs_2_, ...), custom_call_target="tpu_custom_call" | custom-call | flops 1 | bytes 1 | tf_op jit(solution)/shard_map/assemble/pallas_call | solution.py:236
  63.3 2.7 %collective-permute-start.23 = (bf16[128,1024]{1,0:T(8,128)(2,1)S(1)}, bf16[128,1024]{1,0:T(8,128)(2,1)S(1)}, u32[]{:S(2)}, u32[]{:S(2)}) collective-permute-start(bf16[128,1024]{1,0:T(8,128)(2,1)S(1)} %project_other.5), channel_id=1, source_target_pairs={{0,3},{1,2},{2,1},{3,0},{4,7},{5,6},{6,5},{7,4},{8,11},{9,10},{10,... | collective-permute-start | bytes 786440 | tf_op jit(solution)/shard_map/ppermute | solution.py:36
  65.9 2.3 %local_part.7 = (f32[256,1024]{1,0:T(8,128)S(1)}, bf16[256,1024]{1,0:T(8,128)(2,1)S(1)}) custom-call(bf16[1024,1024]{1,0:T(8,128)(2,1)S(1)} %copy-done.2, bf16[1024,1024]{1,0:T(8,128)(2,1)S(1)} %get-tuple-element.67.feat_ref, bf16[1024,1024]{1,0:T(8,128)(2,1)S(1)} %copy-done.1), custom_call_target="tpu_custom_call" | custom-call | flops 1 | bytes 1 | tf_op jit(solution)/shard_map/local_part/pallas_call | solution.py:140
  69.5 2.2 %collective-permute-done.23.refs_9_ = bf16[128,1024]{1,0:T(8,128)(2,1)S(1)} collective-permute-done((bf16[128,1024]{1,0:T(8,128)(2,1)S(1)}, bf16[128,1024]{1,0:T(8,128)(2,1)S(1)}, u32[]{:S(2)}, u32[]{:S(2)}) %collective-permute-start.23) | collective-permute-done | bytes 262176 | tf_op jit(solution)/shard_map/ppermute | solution.py:36
  72.5 2.3 %collective-permute-start.24 = (bf16[128,1024]{1,0:T(8,128)(2,1)S(1)}, bf16[128,1024]{1,0:T(8,128)(2,1)S(1)}, u32[]{:S(2)}, u32[]{:S(2)}) collective-permute-start(bf16[128,1024]{1,0:T(8,128)(2,1)S(1)} %project_other.7), channel_id=1, source_target_pairs={{0,3},{1,2},{2,1},{3,0},{4,7},{5,6},{6,5},{7,4},{8,11},{9,10},{10,... | collective-permute-start | bytes 786440 | tf_op jit(solution)/shard_map/ppermute | solution.py:36
  76.4 2.4 %collective-permute-start.28 = (bf16[2,512,128]{2,1,0:T(8,128)(2,1)S(1)}, bf16[2,512,128]{2,1,0:T(8,128)(2,1)S(1)}, u32[]{:S(2)}, u32[]{:S(2)}) collective-permute-start(bf16[2,512,128]{2,1,0:T(8,128)(2,1)S(1)} %pad_maximum_fusion.2), channel_id=1, source_target_pairs={{0,8},{1,9},{2,10},{3,11},{4,36},{5,37},{6,38},{7,39},{8,16},{9,17... | collective-permute-start | bytes 786440 | tf_op jit(solution)/shard_map/ppermute | solution.py:36
  82.1 2.4 %collective-permute-start.25 = (bf16[256,1024]{1,0:T(8,128)(2,1)S(1)}, bf16[256,1024]{1,0:T(8,128)(2,1)S(1)}, u32[]{:S(2)}, u32[]{:S(2)}) collective-permute-start(bf16[256,1024]{1,0:T(8,128)(2,1)S(1)} %project_other.6), channel_id=1, source_target_pairs={{0,3},{1,2},{2,1},{3,0},{4,7},{5,6},{6,5},{7,4},{8,11},{9,10},{10,... | collective-permute-start | bytes 1572872 | tf_op jit(solution)/shard_map/ppermute | solution.py:36
  87.9 3.0 %collective-permute-start.30 = (bf16[4,2,512,128]{3,2,1,0:T(8,128)(2,1)S(1)}, bf16[4,2,512,128]{3,2,1,0:T(8,128)(2,1)S(1)}, u32[]{:S(2)}, u32[]{:S(2)}) collective-permute-start(bf16[4,2,512,128]{3,2,1,0:T(8,128)(2,1)S(1)} %pad_maximum_fusion.refs_0_), channel_id=1, source_target_pairs={{0,96},{1,97},{2,98},{3,99},{4,28},{5,29},{6,30},{7,31},{8,104},{9... | collective-permute-start | bytes 3145736 | tf_op jit(solution)/shard_map/ppermute | solution.py:36
  92.3 4.3 %collective-permute-done.25.refs_11_ = bf16[256,1024]{1,0:T(8,128)(2,1)S(1)} collective-permute-done((bf16[256,1024]{1,0:T(8,128)(2,1)S(1)}, bf16[256,1024]{1,0:T(8,128)(2,1)S(1)}, u32[]{:S(2)}, u32[]{:S(2)}) %collective-permute-start.25) | collective-permute-done | bytes 524320 | tf_op jit(solution)/shard_map/ppermute | solution.py:36
  97.8 2.6 %collective-permute-start.34 = (bf16[256,1024]{1,0:T(8,128)(2,1)S(1)}, bf16[256,1024]{1,0:T(8,128)(2,1)S(1)}, u32[]{:S(2)}, u32[]{:S(2)}) collective-permute-start(bf16[256,1024]{1,0:T(8,128)(2,1)S(1)} %project_other.8), channel_id=1, source_target_pairs={{0,3},{1,2},{2,1},{3,0},{4,7},{5,6},{6,5},{7,4},{8,11},{9,10},{10,... | collective-permute-start | bytes 1572872 | tf_op jit(solution)/shard_map/ppermute | solution.py:36
  100.4 2.0 %collective-permute-done.19.peer_ref.refs_1_ = bf16[256,1024]{1,0:T(8,128)(2,1)S(1)} collective-permute-done((bf16[256,1024]{1,0:T(8,128)(2,1)S(1)}, bf16[256,1024]{1,0:T(8,128)(2,1)S(1)}, u32[]{:S(2)}, u32[]{:S(2)}) %collective-permute-start.19) | collective-permute-done | bytes 524320 | tf_op jit(solution)/shard_map/ppermute | solution.py:36
  105.3 8.5 %collective-permute-done.31.refs_2_ = bf16[4,2,512,128]{3,2,1,0:T(8,128)(2,1)S(1)} collective-permute-done((bf16[4,2,512,128]{3,2,1,0:T(8,128)(2,1)S(1)}, bf16[4,2,512,128]{3,2,1,0:T(8,128)(2,1)S(1)}, u32[]{:S(2)}, u32[]{:S(2)}) %collective-permute-start.31) | collective-permute-done | bytes 1048608 | tf_op jit(solution)/shard_map/ppermute | solution.py:36
  115.4 4.6 %project_own.2.refs_4_ = bf16[1024,1024]{1,0:T(8,128)(2,1)} custom-call(bf16[128,1024]{1,0:T(8,128)(2,1)S(1)} %norm_part.5.normed_ref.refs_0_, bf16[128,1024]{1,0:T(8,128)(2,1)S(1)} %norm_part.6.normed_ref.refs_1_, bf16[256,1024]{1,0:T(8,128)(2,1)S(1)} %norm_part.7.normed_ref.refs_2_, bf16[256,1024]{1,0:T(8,128)(2,1)S(1)} %norm_part.8.normed_ref.refs_3_, ...), custom_call_target="tpu_custom_call" | custom-call | flops 1 | bytes 1 | tf_op jit(solution)/shard_map/project_own/pallas_call | solution.py:305
  120.0 2.7 %collective-permute-done.33.refs_3_ = bf16[256,1024]{1,0:T(8,128)(2,1)S(1)} collective-permute-done((bf16[256,1024]{1,0:T(8,128)(2,1)S(1)}, bf16[256,1024]{1,0:T(8,128)(2,1)S(1)}, u32[]{:S(2)}, u32[]{:S(2)}) %collective-permute-start.33) | collective-permute-done | bytes 524320 | tf_op jit(solution)/shard_map/ppermute | solution.py:36
  122.7 2.0 %project_own.3 = bf16[1024,1024]{1,0:T(8,128)(2,1)} custom-call(bf16[256,1024]{1,0:T(8,128)(2,1)S(1)} %norm_part.9.normed_ref.refs_0_, bf16[256,1024]{1,0:T(8,128)(2,1)S(1)} %collective-permute-done.19.peer_ref.refs_1_, bf16[2,1024,1024]{2,1,0:T(8,128)(2,1)S(1)} %assemble.3.refs_8_.refs_2_, ...), custom_call_target="tpu_custom_call", output_to_operand_aliasing={{}: (4, {})} | custom-call | flops 1 | bytes 1 | tf_op jit(solution)/shard_map/project_own/pallas_call | solution.py:305
  (86 shorter events, 45.4 us)
Async XLA Ops:
  9.4 8.6 %collective-permute-start.4 = (bf16[512,128]{1,0:T(8,128)(2,1)S(1)}, bf16[512,128]{1,0:T(8,128)(2,1)S(1)}, u32[]{:S(2)}, u32[]{:S(2)}) collective-permute-start(bf16[512,128]{1,0:T(8,128)(2,1)S(1)} %get-tuple-element.123), channel_id=1, source_target_pairs={{0,96},{1,64},{2,67},{3,99},{4,100},{5,68},{6,71},{7,103},{8,104},... | collective-permute-start | bytes 393224 | tf_op jit(solution)/shard_map/ppermute | solution.py:36
  22.1 8.8 %collective-permute-start.5 = (bf16[4,128,128]{2,1,0:T(8,128)(2,1)S(1)}, bf16[4,128,128]{2,1,0:T(8,128)(2,1)S(1)}, u32[]{:S(2)}, u32[]{:S(2)}) collective-permute-start(bf16[4,128,128]{2,1,0:T(8,128)(2,1)S(1)} %get-tuple-element.82), channel_id=1, source_target_pairs={{0,32},{1,33},{2,34},{3,35},{4,36},{5,37},{6,38},{7,39},{8,40},{9,... | collective-permute-start | bytes 393224 | tf_op jit(solution)/shard_map/ppermute | solution.py:36
  34.2 13.3 %collective-permute-start.14 = (bf16[4,512,128]{2,1,0:T(8,128)(2,1)S(1)}, bf16[4,512,128]{2,1,0:T(8,128)(2,1)S(1)}, u32[]{:S(2)}, u32[]{:S(2)}) collective-permute-start(bf16[4,512,128]{2,1,0:T(8,128)(2,1)S(1)} %pad_maximum_fusion.1.refs_0_), channel_id=1, source_target_pairs={{0,64},{1,65},{2,66},{3,67},{4,20},{5,21},{6,22},{7,23},{8,72},{9,... | collective-permute-start | bytes 1572872 | tf_op jit(solution)/shard_map/ppermute | solution.py:36
  35.6 15.0 %collective-permute-start.13 = (bf16[4,512,128]{2,1,0:T(8,128)(2,1)S(1)}, bf16[4,512,128]{2,1,0:T(8,128)(2,1)S(1)}, u32[]{:S(2)}, u32[]{:S(2)}) collective-permute-start(bf16[4,512,128]{2,1,0:T(8,128)(2,1)S(1)} %pad_maximum_fusion.1.refs_0_), channel_id=1, source_target_pairs={{0,32},{1,33},{2,34},{3,35},{4,12},{5,13},{6,14},{7,15},{8,40},{9,... | collective-permute-start | bytes 1572872 | tf_op jit(solution)/shard_map/ppermute | solution.py:36
  36.0 14.6 %collective-permute-start.12 = (bf16[4,512,128]{2,1,0:T(8,128)(2,1)S(1)}, bf16[4,512,128]{2,1,0:T(8,128)(2,1)S(1)}, u32[]{:S(2)}, u32[]{:S(2)}) collective-permute-start(bf16[4,512,128]{2,1,0:T(8,128)(2,1)S(1)} %pad_maximum_fusion.1.refs_0_), channel_id=1, source_target_pairs={{0,96},{1,97},{2,98},{3,99},{4,28},{5,29},{6,30},{7,31},{8,104},{9... | collective-permute-start | bytes 1572872 | tf_op jit(solution)/shard_map/ppermute | solution.py:36
  40.8 9.8 %collective-permute-start.11 = (bf16[128,1024]{1,0:T(8,128)(2,1)S(1)}, bf16[128,1024]{1,0:T(8,128)(2,1)S(1)}, u32[]{:S(2)}, u32[]{:S(2)}) collective-permute-start(bf16[128,1024]{1,0:T(8,128)(2,1)S(1)} %norm_part.5.normed_ref.refs_0_), channel_id=1, source_target_pairs={{0,1},{1,0},{2,3},{3,2},{4,5},{5,4},{6,7},{7,6},{8,9},{9,8},{10,11... | collective-permute-start | bytes 786440 | tf_op jit(solution)/shard_map/ppermute | solution.py:36
  50.6 10.0 %collective-permute-start.15 = (bf16[4,512,128]{2,1,0:T(8,128)(2,1)S(1)}, bf16[4,512,128]{2,1,0:T(8,128)(2,1)S(1)}, u32[]{:S(2)}, u32[]{:S(2)}) collective-permute-start(bf16[4,512,128]{2,1,0:T(8,128)(2,1)S(1)} %pad_maximum_fusion.1.refs_0_), channel_id=1, source_target_pairs={{0,4},{1,5},{2,6},{3,7},{4,0},{5,1},{6,2},{7,3},{8,12},{9,13},{10,... | collective-permute-start | bytes 1572872 | tf_op jit(solution)/shard_map/ppermute | solution.py:36
  50.6 10.0 %collective-permute-start.16 = (bf16[4,512,128]{2,1,0:T(8,128)(2,1)S(1)}, bf16[4,512,128]{2,1,0:T(8,128)(2,1)S(1)}, u32[]{:S(2)}, u32[]{:S(2)}) collective-permute-start(bf16[4,512,128]{2,1,0:T(8,128)(2,1)S(1)} %collective-permute-done.12.refs_1_), channel_id=1, source_target_pairs={{0,4},{1,5},{2,6},{3,7},{4,0},{5,1},{6,2},{7,3},{8,12},{9,13},{10,... | collective-permute-start | bytes 1572872 | tf_op jit(solution)/shard_map/ppermute | solution.py:36
  51.1 9.5 %collective-permute-start.17 = (bf16[4,512,128]{2,1,0:T(8,128)(2,1)S(1)}, bf16[4,512,128]{2,1,0:T(8,128)(2,1)S(1)}, u32[]{:S(2)}, u32[]{:S(2)}) collective-permute-start(bf16[4,512,128]{2,1,0:T(8,128)(2,1)S(1)} %collective-permute-done.13.refs_2_), channel_id=1, source_target_pairs={{0,4},{1,5},{2,6},{3,7},{4,0},{5,1},{6,2},{7,3},{8,12},{9,13},{10,... | collective-permute-start | bytes 1572872 | tf_op jit(solution)/shard_map/ppermute | solution.py:36
  51.2 9.5 %collective-permute-start.18 = (bf16[4,512,128]{2,1,0:T(8,128)(2,1)S(1)}, bf16[4,512,128]{2,1,0:T(8,128)(2,1)S(1)}, u32[]{:S(2)}, u32[]{:S(2)}) collective-permute-start(bf16[4,512,128]{2,1,0:T(8,128)(2,1)S(1)} %collective-permute-done.14.refs_3_), channel_id=1, source_target_pairs={{0,4},{1,5},{2,6},{3,7},{4,0},{5,1},{6,2},{7,3},{8,12},{9,13},{10,... | collective-permute-start | bytes 1572872 | tf_op jit(solution)/shard_map/ppermute | solution.py:36
  51.6 8.3 %collective-permute-start.21 = (bf16[128,1024]{1,0:T(8,128)(2,1)S(1)}, bf16[128,1024]{1,0:T(8,128)(2,1)S(1)}, u32[]{:S(2)}, u32[]{:S(2)}) collective-permute-start(bf16[128,1024]{1,0:T(8,128)(2,1)S(1)} %norm_part.6.normed_ref.refs_1_), channel_id=1, source_target_pairs={{0,1},{1,0},{2,3},{3,2},{4,5},{5,4},{6,7},{7,6},{8,9},{9,8},{10,11... | collective-permute-start | bytes 786440 | tf_op jit(solution)/shard_map/ppermute | solution.py:36
  59.9 18.9 %collective-permute-start.22 = (bf16[256,1024]{1,0:T(8,128)(2,1)S(1)}, bf16[256,1024]{1,0:T(8,128)(2,1)S(1)}, u32[]{:S(2)}, u32[]{:S(2)}) collective-permute-start(bf16[256,1024]{1,0:T(8,128)(2,1)S(1)} %norm_part.7.normed_ref.refs_2_), channel_id=1, source_target_pairs={{0,1},{1,0},{2,3},{3,2},{4,5},{5,4},{6,7},{7,6},{8,9},{9,8},{10,11... | collective-permute-start | bytes 1572872 | tf_op jit(solution)/shard_map/ppermute | solution.py:36
  63.3 8.5 %collective-permute-start.23 = (bf16[128,1024]{1,0:T(8,128)(2,1)S(1)}, bf16[128,1024]{1,0:T(8,128)(2,1)S(1)}, u32[]{:S(2)}, u32[]{:S(2)}) collective-permute-start(bf16[128,1024]{1,0:T(8,128)(2,1)S(1)} %project_other.5), channel_id=1, source_target_pairs={{0,3},{1,2},{2,1},{3,0},{4,7},{5,6},{6,5},{7,4},{8,11},{9,10},{10,... | collective-permute-start | bytes 786440 | tf_op jit(solution)/shard_map/ppermute | solution.py:36
  71.7 19.1 %collective-permute-start.20 = (bf16[256,1024]{1,0:T(8,128)(2,1)S(1)}, bf16[256,1024]{1,0:T(8,128)(2,1)S(1)}, u32[]{:S(2)}, u32[]{:S(2)}) collective-permute-start(bf16[256,1024]{1,0:T(8,128)(2,1)S(1)} %norm_part.8.normed_ref.refs_3_), channel_id=1, source_target_pairs={{0,1},{1,0},{2,3},{3,2},{4,5},{5,4},{6,7},{7,6},{8,9},{9,8},{10,11... | collective-permute-start | bytes 1572872 | tf_op jit(solution)/shard_map/ppermute | solution.py:36
  72.5 9.6 %collective-permute-start.24 = (bf16[128,1024]{1,0:T(8,128)(2,1)S(1)}, bf16[128,1024]{1,0:T(8,128)(2,1)S(1)}, u32[]{:S(2)}, u32[]{:S(2)}) collective-permute-start(bf16[128,1024]{1,0:T(8,128)(2,1)S(1)} %project_other.7), channel_id=1, source_target_pairs={{0,3},{1,2},{2,1},{3,0},{4,7},{5,6},{6,5},{7,4},{8,11},{9,10},{10,... | collective-permute-start | bytes 786440 | tf_op jit(solution)/shard_map/ppermute | solution.py:36
  74.9 9.7 %collective-permute-start.29 = (bf16[2,512,128]{2,1,0:T(8,128)(2,1)S(1)}, bf16[2,512,128]{2,1,0:T(8,128)(2,1)S(1)}, u32[]{:S(2)}, u32[]{:S(2)}) collective-permute-start(bf16[2,512,128]{2,1,0:T(8,128)(2,1)S(1)} %pad_maximum_fusion.2), channel_id=1, source_target_pairs={{0,16},{1,17},{2,18},{3,19},{4,68},{5,69},{6,70},{7,71},{8,24},{9,... | collective-permute-start | bytes 786440 | tf_op jit(solution)/shard_map/ppermute | solution.py:36
  76.4 9.2 %collective-permute-start.28 = (bf16[2,512,128]{2,1,0:T(8,128)(2,1)S(1)}, bf16[2,512,128]{2,1,0:T(8,128)(2,1)S(1)}, u32[]{:S(2)}, u32[]{:S(2)}) collective-permute-start(bf16[2,512,128]{2,1,0:T(8,128)(2,1)S(1)} %pad_maximum_fusion.2), channel_id=1, source_target_pairs={{0,8},{1,9},{2,10},{3,11},{4,36},{5,37},{6,38},{7,39},{8,16},{9,17... | collective-permute-start | bytes 786440 | tf_op jit(solution)/shard_map/ppermute | solution.py:36
  82.1 14.4 %collective-permute-start.25 = (bf16[256,1024]{1,0:T(8,128)(2,1)S(1)}, bf16[256,1024]{1,0:T(8,128)(2,1)S(1)}, u32[]{:S(2)}, u32[]{:S(2)}) collective-permute-start(bf16[256,1024]{1,0:T(8,128)(2,1)S(1)} %project_other.6), channel_id=1, source_target_pairs={{0,3},{1,2},{2,1},{3,0},{4,7},{5,6},{6,5},{7,4},{8,11},{9,10},{10,... | collective-permute-start | bytes 1572872 | tf_op jit(solution)/shard_map/ppermute | solution.py:36
  86.1 19.1 %collective-permute-start.32 = (bf16[4,2,512,128]{3,2,1,0:T(8,128)(2,1)S(1)}, bf16[4,2,512,128]{3,2,1,0:T(8,128)(2,1)S(1)}, u32[]{:S(2)}, u32[]{:S(2)}) collective-permute-start(bf16[4,2,512,128]{3,2,1,0:T(8,128)(2,1)S(1)} %pad_maximum_fusion.refs_0_), channel_id=1, source_target_pairs={{0,64},{1,65},{2,66},{3,67},{4,20},{5,21},{6,22},{7,23},{8,72},{9,... | collective-permute-start | bytes 3145736 | tf_op jit(solution)/shard_map/ppermute | solution.py:36
  87.6 26.1 %collective-permute-start.31 = (bf16[4,2,512,128]{3,2,1,0:T(8,128)(2,1)S(1)}, bf16[4,2,512,128]{3,2,1,0:T(8,128)(2,1)S(1)}, u32[]{:S(2)}, u32[]{:S(2)}) collective-permute-start(bf16[4,2,512,128]{3,2,1,0:T(8,128)(2,1)S(1)} %pad_maximum_fusion.refs_0_), channel_id=1, source_target_pairs={{0,32},{1,33},{2,34},{3,35},{4,12},{5,13},{6,14},{7,15},{8,40},{9,... | collective-permute-start | bytes 3145736 | tf_op jit(solution)/shard_map/ppermute | solution.py:36
  87.9 25.9 %collective-permute-start.30 = (bf16[4,2,512,128]{3,2,1,0:T(8,128)(2,1)S(1)}, bf16[4,2,512,128]{3,2,1,0:T(8,128)(2,1)S(1)}, u32[]{:S(2)}, u32[]{:S(2)}) collective-permute-start(bf16[4,2,512,128]{3,2,1,0:T(8,128)(2,1)S(1)} %pad_maximum_fusion.refs_0_), channel_id=1, source_target_pairs={{0,96},{1,97},{2,98},{3,99},{4,28},{5,29},{6,30},{7,31},{8,104},{9... | collective-permute-start | bytes 3145736 | tf_op jit(solution)/shard_map/ppermute | solution.py:36
  90.8 11.6 %collective-permute-start.19 = (bf16[256,1024]{1,0:T(8,128)(2,1)S(1)}, bf16[256,1024]{1,0:T(8,128)(2,1)S(1)}, u32[]{:S(2)}, u32[]{:S(2)}) collective-permute-start(bf16[256,1024]{1,0:T(8,128)(2,1)S(1)} %norm_part.9.normed_ref.refs_0_), channel_id=1, source_target_pairs={{0,1},{1,0},{2,3},{3,2},{4,5},{5,4},{6,7},{7,6},{8,9},{9,8},{10,11... | collective-permute-start | bytes 1572872 | tf_op jit(solution)/shard_map/ppermute | solution.py:36
  97.8 17.5 %collective-permute-start.34 = (bf16[256,1024]{1,0:T(8,128)(2,1)S(1)}, bf16[256,1024]{1,0:T(8,128)(2,1)S(1)}, u32[]{:S(2)}, u32[]{:S(2)}) collective-permute-start(bf16[256,1024]{1,0:T(8,128)(2,1)S(1)} %project_other.8), channel_id=1, source_target_pairs={{0,3},{1,2},{2,1},{3,0},{4,7},{5,6},{6,5},{7,4},{8,11},{9,10},{10,... | collective-permute-start | bytes 1572872 | tf_op jit(solution)/shard_map/ppermute | solution.py:36
  103.7 19.0 %collective-permute-start.33 = (bf16[256,1024]{1,0:T(8,128)(2,1)S(1)}, bf16[256,1024]{1,0:T(8,128)(2,1)S(1)}, u32[]{:S(2)}, u32[]{:S(2)}) collective-permute-start(bf16[256,1024]{1,0:T(8,128)(2,1)S(1)} %project_other.9), channel_id=1, source_target_pairs={{0,3},{1,2},{2,1},{3,0},{4,7},{5,6},{6,5},{7,4},{8,11},{9,10},{10,... | collective-permute-start | bytes 1572872 | tf_op jit(solution)/shard_map/ppermute | solution.py:36
  (16 other events, 88.3 us)
